TPU v7x, 256 devices: a whole 4x4x8 slice. The times are simulated.
256 devices in a mesh: seq: 64 (over y_hi, z, x), blk: 4 (over y_lo, core).
Axes of the slice: x: 4, y: 4 (y_hi: 2, y_lo: 2; y = y_hi * 2 + y_lo), z: 8, core: 2. Of those that a mesh axis runs over, the one named last changes fastest.
Arguments:
- lin_query: bfloat16 [8192, 4096], P('seq', 'blk'), may hold values from -6 to 6
- lin_key: bfloat16 [8192, 4096], P('seq', 'blk'), may hold values from -6 to 6
- lin_value: bfloat16 [8192, 4096], P('seq', 'blk'), may hold values from -6 to 6
- log_decay: float32 [32, 8192], P('blk', 'seq'), may hold values from -1.5 to 0, as said below
- norm_gain: float32 [4096], P('blk'), may hold values from 0.1 to 1.9
- soft_query: bfloat16 [8192, 4096], P('seq', 'blk'), may hold values from -60 to 60
- span_kv: bfloat16 [8192, 2, 4, 128], P('seq', None, 'blk'), may hold values from -6 to 6
- cache_kv: bfloat16 [4096, 2, 4, 128], P('blk'), may hold values from -6 to 6
- cache_lens: int32 [4], replicated, may hold values from 1 to 1024, 3072 in all
- span_start: int32 [1], replicated, may hold values from 3072 to 7167
Outputs:
- linear_out: bfloat16 [8192, 4096], P('seq', 'blk')
- attended: bfloat16 [8192, 4096], P('seq', 'blk')
Inputs may be any that keep to these rules, and one draw needn't show every extreme that they name: `log_decay`: every entry is below zero. Slots 0 to cache_lens[b] - 1 of shard b hold the cached prefix; the shard's later slots are empty.
All inputs are finite; a program needn't handle non-finite values.
Results may differ from a plain program's by a relative error of at most 0.029.
Values may be sent and summed in bfloat16 or wider, within the bound.
A program may use at most 128 MiB of HBM per device.

v0:
```python
import math

import jax
import jax.numpy as jnp
import numpy as np
from jax import lax
from jax.sharding import PartitionSpec as P

rotary_rates = (10000000.0 ** (-np.arange(32) / 32.0)).astype(np.float32)
epsilon = 1e-06
highest = lax.Precision.HIGHEST
score_scale = 1.0 / math.sqrt(128.0)


def prefix(array, axis, join, neutral):
    place = lax.axis_index(axis)
    gathered = jax.tree.map(
        lambda a, kind: lax.all_gather(a.astype(kind), axis), array, (jnp.bfloat16, jnp.bfloat16)
    )
    state = jax.tree.map(lambda a, e: jnp.zeros_like(a) + jnp.asarray(e, a.dtype), array, neutral)

    def one(step, state):
        return join(
            state,
            jax.tree.map(
                lambda a, own: lax.dynamic_index_in_dim(a, step, 0, False).astype(own.dtype),
                gathered,
                array,
            ),
        )

    return lax.fori_loop(0, place, one, state)


def rotate(features, positions):
    angles = positions[:, None] * jnp.asarray(rotary_rates)[None, :]
    cosine = jnp.cos(angles)[:, None, :]
    sine_term = jnp.sin(angles)[:, None, :]
    leading = features[:, :, :32]
    trailing = features[:, :, 32:64]
    return jnp.concatenate(
        [
            leading * cosine - trailing * sine_term,
            trailing * cosine + leading * sine_term,
            features[:, :, 64:],
        ],
        axis=2,
    )


def normalize(outputs, norm_gain):
    root_mean = jnp.sqrt(jnp.mean(outputs * outputs, axis=2, keepdims=True) + epsilon)
    scaled = outputs / root_mean * norm_gain.reshape(1, outputs.shape[1], outputs.shape[2])
    return scaled.reshape(outputs.shape[0], outputs.shape[1] * outputs.shape[2]).astype(
        jnp.bfloat16
    )


def lightning_terms(queries, key_rows, value_rows, decays):
    cumulative = jnp.cumsum(decays, axis=1)
    length = queries.shape[0]
    positions = jnp.arange(length, dtype=jnp.int32)
    causal = positions[:, None] >= positions[None, :]
    scores = jnp.einsum("thd,uhd->htu", queries, key_rows, preferred_element_type=jnp.float32)
    differences = cumulative[:, :, None] - cumulative[:, None, :]
    weights = jnp.where(causal[None], jnp.exp(jnp.minimum(differences, 0.0)), 0.0)
    values_wide = value_rows.astype(jnp.float32)
    within = jnp.einsum("htu,uhd->thd", scores * weights, values_wide, precision=highest)
    tail_decay = jnp.exp(cumulative[:, -1:] - cumulative).T[:, :, None]
    local_state = jnp.einsum(
        "thd,the->hde", key_rows.astype(jnp.float32) * tail_decay, values_wide, precision=highest
    )
    return (within, local_state, cumulative)


def empty_state(kv_count, group_size, token_count, head_width):
    return (
        jnp.full((kv_count, group_size, token_count), -1e30, jnp.float32),
        jnp.zeros((kv_count, group_size, token_count), jnp.float32),
        jnp.zeros((kv_count, group_size, token_count, head_width), jnp.float32),
    )


def attend(running, grouped, key_block, value_block, allowed):
    old_peak, weight_sum, weighted = running
    scores = (
        jnp.einsum("tkgd,ukd->kgtu", grouped, key_block, preferred_element_type=jnp.float32)
        * score_scale
    )
    visible = allowed[None, None]
    new_peak = jnp.maximum(old_peak, jnp.max(jnp.where(visible, scores, -1e30), axis=-1))
    shrink = jnp.exp(old_peak - new_peak)
    weights = jnp.where(visible, jnp.exp(scores - new_peak[..., None]), 0.0)
    weight_sum = weight_sum * shrink + jnp.sum(weights, axis=-1)
    update = jnp.einsum(
        "kgtu,ukd->kgtd",
        weights.astype(jnp.bfloat16),
        value_block,
        preferred_element_type=jnp.float32,
    )
    weighted = weighted * shrink[..., None] + update
    return (new_peak, weight_sum, weighted)


def fold_keys(running, grouped, key_value, allowed):
    row_total = key_value.shape[0]
    block_rows = 1024

    def advance(carry_state, offset):
        kv_block = lax.dynamic_slice_in_dim(key_value, offset, block_rows, 0)
        return (
            attend(
                carry_state, grouped, kv_block[:, 0], kv_block[:, 1], allowed(offset, block_rows)
            ),
            None,
        )

    offsets = jnp.arange(row_total // block_rows, dtype=jnp.int32) * block_rows
    running, _ = lax.scan(advance, running, offsets)
    return running


def per_device(
    lin_query,
    lin_key,
    lin_value,
    log_decay,
    norm_gain,
    soft_query,
    span_kv,
    cache_kv,
    cache_lens,
    span_start,
):
    token_count = lin_query.shape[0]
    heads_here = log_decay.shape[0]
    head_width = lin_query.shape[1] // heads_here
    query_heads = lin_query.reshape(token_count, heads_here, head_width)
    key_heads = lin_key.reshape(token_count, heads_here, head_width)
    value_heads = lin_value.reshape(token_count, heads_here, head_width)
    within, local_state, cumulative = lightning_terms(
        query_heads, key_heads, value_heads, log_decay
    )

    def combine(earlier, following):
        return (earlier[0] * following[0], following[0][:, None, None] * earlier[1] + following[1])

    identity = (jnp.ones((heads_here,), jnp.float32), jnp.zeros_like(local_state))
    _, incoming = prefix((jnp.exp(cumulative[:, -1]), local_state), "seq", combine, identity)
    scaled = query_heads.astype(jnp.float32) * jnp.exp(cumulative).T[:, :, None]
    carried = jnp.einsum("thd,hde->the", scaled, incoming, precision=highest)
    linear_out = normalize(within + carried, norm_gain)
    first_row = lax.axis_index("seq") * token_count
    positions = (span_start[0] + first_row + jnp.arange(token_count, dtype=jnp.int32)).astype(
        jnp.float32
    )
    combined = soft_query.astype(jnp.float32) + linear_out.astype(jnp.float32)
    queries = rotate(combined.reshape(token_count, heads_here, head_width), positions).astype(
        jnp.bfloat16
    )
    kv_here = span_kv.shape[2]
    group_size = heads_here // kv_here
    span_keys = rotate(span_kv[:, 0].astype(jnp.float32), positions).astype(jnp.bfloat16)
    span_pair = jnp.stack([span_keys, span_kv[:, 1]], axis=1)
    grouped = queries.reshape(token_count, kv_here, group_size, head_width)
    query_index = first_row + jnp.arange(token_count, dtype=jnp.int32)

    def span_step(running, shard_rows):

        def allowed(offset, block_rows):
            key_index = offset + jnp.arange(block_rows, dtype=jnp.int32)
            return query_index[:, None] >= key_index[None, :]

        return fold_keys(running, grouped, shard_rows, allowed)

    running = span_step(
        empty_state(kv_here, group_size, token_count, head_width),
        lax.all_gather(span_pair, "seq", axis=0, tiled=True),
    )
    capacity = cache_kv.shape[0]
    shard_count = lax.axis_size("blk")
    shard_ids = jnp.arange(shard_count, dtype=jnp.int32)
    head_cache = lax.all_to_all(cache_kv, "blk", split_axis=2, concat_axis=0, tiled=True)

    def cache_allowed(offset, block_rows):
        slot_index = offset + jnp.arange(block_rows, dtype=jnp.int32)
        slot_limit = jnp.sum(
            jnp.where(
                (slot_index // capacity)[:, None] == shard_ids[None, :], cache_lens[None, :], 0
            ),
            axis=1,
        )
        return (slot_index % capacity < slot_limit)[None, :]

    new_peak, weight_sum, weighted = fold_keys(running, grouped, head_cache, cache_allowed)
    result = (weighted / weight_sum[..., None]).transpose(2, 0, 1, 3)
    attended = result.reshape(token_count, heads_here * head_width).astype(jnp.bfloat16)
    return (linear_out, attended)


def solution(mesh):
    in_specs = (
        P("seq", "blk"),
        P("seq", "blk"),
        P("seq", "blk"),
        P("blk", "seq"),
        P("blk"),
        P("seq", "blk"),
        P("seq", None, "blk", None),
        P("blk", None, None, None),
        P(),
        P(),
    )
    out_specs = (P("seq", "blk"), P("seq", "blk"))
    return jax.shard_map(
        per_device, mesh=mesh, in_specs=in_specs, out_specs=out_specs, check_vma=False
    )
```

profile of v0, /device:TPU:16, one launch (start us, length us, event | category | flops | bytes accessed | tf_op | source)
XLA Modules:
  0.0 478.5 jit_solution(229707376546934854)
XLA Ops:
  8.5 1.1 copy.142
  9.6 2.1 convolution_convert_fusion
  15.2 3.2 copy.128
  18.5 3.6 all-to-all-start
  23.9 186.6 %all-reduce = bf16[512]{0:T(512)(128)(2,1)S(1)} all-reduce(bf16[512]{0:T(512)(128)(2,1)S(1)} %dynamic-update-slice), channel_id=2, replica_groups=mesh['seq'=64,'blk'=4] {'seq'}, use_global_device_ids=true, to_apply=%add | all-reduce | flops 512 | bytes 2048
  211.9 1.5 copy.129
  213.4 37.1 %while.44 = (s32[]{:T(128)}, f32[8,128,128]{2,1,0:T(8,128)S(1)}, s32[]{:T(128)}, bf16[64,8]{1,0:T(8,128)(2,1)S(1)}, bf16[64,8,128,128]{3,2,1,0:T(8,128)(2,1)}, /*index=5*/s32[]{:T(128)}, s32[]{:T(128)}, s32[]{:T(128)}) while((s32[]{:T(128)}, f32[8,128,128]{2,1,0:T(8,128)S(1)}, s32[]{:T(128)}, bf16[64,8]{1,0:T(8,128)(2,1)S(1)}, ...), condition=%wide.region_2.3_spmd, body=%wide.region_1.2_spmd.sunk | while | flops 393229 | bytes 1310927 | solution.py:32
  213.5 1.1 convert_add_fusion.3
  214.6 1.1 convert_add_fusion.3
  215.8 1.1 convert_add_fusion.3
  216.9 1.1 convert_add_fusion.3
  218.1 1.1 convert_add_fusion.3
  219.3 1.1 convert_add_fusion.3
  220.4 1.1 convert_add_fusion.3
  221.6 1.1 convert_add_fusion.3
  222.7 1.1 convert_add_fusion.3
  223.9 1.1 convert_add_fusion.3
  225.0 1.1 convert_add_fusion.3
  226.2 1.1 convert_add_fusion.3
  227.3 1.1 convert_add_fusion.3
  228.5 1.1 convert_add_fusion.3
  229.7 1.1 convert_add_fusion.3
  230.8 1.1 convert_add_fusion.3
  232.0 1.1 convert_add_fusion.3
  233.1 1.1 convert_add_fusion.3
  234.3 1.1 convert_add_fusion.3
  235.4 1.1 convert_add_fusion.3
  236.6 1.1 convert_add_fusion.3
  237.7 1.1 convert_add_fusion.3
  238.9 1.1 convert_add_fusion.3
  240.0 1.1 convert_add_fusion.3
  242.4 1.1 convert_add_fusion.3
  243.5 1.1 convert_add_fusion.3
  244.7 1.1 convert_add_fusion.3
  245.8 1.1 convert_add_fusion.3
  247.0 1.1 convert_add_fusion.3
  250.6 1.3 multiply_reduce_fusion
  252.5 72.9 %all-gather.5.cloned.1.call-done = bf16[8192,2,1,128]{0,3,2,1:T(8,128)(2,1)} async-done(((bf16[128,2,1,128]{0,3,2,1:T(8,128)(2,1)}), bf16[8192,2,1,128]{0,3,2,1:T(8,128)(2,1)}) %all-gather.5.cloned.1.call-update) | async-done | bytes 4194320 | tf_op jit(solution)/shard_map/all_gather | solution.py:178
  325.4 95.8 %while.46 = (s32[]{:T(128)}, f32[1,8,128]{2,1,0:T(8,128)S(1)}, f32[1,8,128]{2,1,0:T(8,128)S(1)}, f32[1,8,128,128]{3,2,1,0:T(8,128)S(1)}, s32[8]{0:T(128)S(1)}, /...) while((s32[]{:T(128)}, f32[1,8,128]{2,1,0:T(8,128)S(1)}, ...), condition=%wide.region_7.8_spmd.clone, body=%wide.region_4.7_spmd.clone.sunk | while | flops 548936832 | bytes 31794408 | solution.py:119
  328.8 3.9 fusion.110
  332.7 3.7 fusion.113
  340.8 3.9 fusion.110
  344.7 3.7 fusion.113
  352.7 3.9 fusion.110
  356.7 3.7 fusion.113
  364.7 3.9 fusion.110
  368.6 3.7 fusion.113
  376.7 3.9 fusion.110
  380.6 3.7 fusion.113
  388.7 3.9 fusion.110
  392.6 3.7 fusion.113
  400.6 3.9 fusion.110
  404.6 3.7 fusion.113
  412.6 3.9 fusion.110
  416.5 3.7 fusion.113
  421.1 48.5 %while.45 = (s32[]{:T(128)}, f32[1,8,128]{2,1,0:T(8,128)S(1)}, f32[1,8,128]{2,1,0:T(8,128)S(1)}, f32[1,8,128,128]{3,2,1,0:T(8,128)S(1)}, s32[4]{0:T(128)S(1)}, /...) while((s32[]{:T(128)}, f32[1,8,128]{2,1,0:T(8,128)S(1)}, ...), condition=%wide.region_12.13_spmd.clone, body=%wide.region_8.12_spmd.clone.sunk | while | flops 548711424 | bytes 31281392 | solution.py:119
  425.1 3.6 fusion.105
  428.7 3.6 fusion.108
  437.2 3.6 fusion.105
  440.9 3.6 fusion.108
  449.4 3.6 fusion.105
  453.0 3.6 fusion.108
  461.5 3.6 fusion.105
  465.1 3.6 fusion.108
  (215 shorter events, 43.0 us)
Async XLA Ops:
  7.2 203.8 %copy-start = (bf16[128,1024]{1,0:T(8,128)(2,1)S(1)}, bf16[128,1024]{1,0:T(8,128)(2,1)}, u32[]{:S(2)}) copy-start(bf16[128,1024]{1,0:T(8,128)(2,1)} %param.17) | copy-start | bytes 786436
  7.2 206.2 %all-gather.7.cloned.1.call-start = ((), (), s32[]{:S(2)}) async-start(), calls=%async_computation.2 | async-start | bytes 17039360 | tf_op jit(solution)/shard_map/all_gather | solution.py:18
  11.7 313.7 %all-gather.5.cloned.1.call-start = ((), (), s32[]{:S(2)}) async-start(), calls=%async_computation.1 | async-start | bytes 4259840 | tf_op jit(solution)/shard_map/all_gather | solution.py:178
  15.2 6.9 %copy-start.9 = (u32[256]{0:T(256)S(1)}, u32[256]{0:T(256)}, u32[]{:S(2)}) copy-start(u32[256]{0:T(256)} %constant.144) | copy-start | bytes 3076
  15.2 195.4 %copy-start.5 = (bf16[128,1024]{1,0:T(8,128)(2,1)S(1)}, bf16[128,1024]{1,0:T(8,128)(2,1)}, u32[]{:S(2)}) copy-start(bf16[128,1024]{1,0:T(8,128)(2,1)} %param.22) | copy-start | bytes 786436
  15.2 195.6 %copy-start.8 = (f32[32]{0:T(128)S(1)}, f32[32]{0:T(128)}, u32[]{:S(2)}) copy-start(f32[32]{0:T(128)} %constant.140.clone) | copy-start | bytes 388
  15.2 196.0 %copy-start.3 = (bf16[128,1024]{1,0:T(8,128)(2,1)S(1)}, bf16[128,1024]{1,0:T(8,128)(2,1)}, u32[]{:S(2)}) copy-start(bf16[128,1024]{1,0:T(8,128)(2,1)} %param.19) | copy-start | bytes 786436
  18.5 193.4 %all-to-all-start = ((bf16[1024,2,4,128]{3,0,1,2:T(8,128)(2,1)}), bf16[1024,2,4,128]{3,0,1,2:T(8,128)(2,1)S(1)}, u32[]{:S(2)}, u32[]{:S(2)}) async-start(bf16[1024,2,4,128]{3,0,1,2:T(8,128)(2,1)} %copy.128), calls=%async_computation | async-start | bytes 4194304 | tf_op jit(solution)/shard_map/all_to_all | solution.py:183
  213.4 38.4 %copy-start.7 = (f32[1024]{0:T(1024)S(1)}, f32[1024]{0:T(1024)}, u32[]{:S(2)}) copy-start(f32[1024]{0:T(1024)} %param.21) | copy-start | bytes 12292
  250.6 74.8 %copy-start.4 = (f32[1,8,128,128]{3,2,1,0:T(8,128)S(1)}, f32[1,8,128,128]{3,2,1,0:T(8,128)}, u32[]{:S(2)}) copy-start(f32[1,8,128,128]{3,2,1,0:T(8,128)} %custom-call.2) | copy-start | bytes 1572868
  325.4 95.8 %copy-start.6 = (s32[4]{0:T(128)S(1)}, s32[4]{0:T(128)}, u32[]{:S(2)}) copy-start(s32[4]{0:T(128)} %param.25) | copy-start | bytes 52
  332.7 3.7 copy-start.1
  344.7 3.7 copy-start.1
  356.7 3.7 copy-start.1
  368.6 3.7 copy-start.1
  380.6 3.7 copy-start.1
  392.6 3.7 copy-start.1
  404.6 3.7 copy-start.1
  416.5 3.7 copy-start.1
  428.7 3.6 copy-start.2
  440.9 3.6 copy-start.2
  453.0 3.6 copy-start.2
  465.1 3.6 copy-start.2
Sparse Core Ops, SparseCore 0:
  12.2 200.4 all-gather.6
  216.7 108.6 all-gather.4
where the time goes:
time: 483 us; the launch traced here: 479 us
  blocking collectives  187 us (39%)
  matrix products  94.3 us (20%)
  waiting for transfers between devices  72.9 us (15%)
  other arithmetic  62.3 us (13%)
  loops' own time  25.4 us (5%)
  local copies, waits for them, and re-layouts  17.6 us (4%)
  between operations  15.7 us (3%)
    unnamed x1, blocking collectives  187 us
    all_gather x1, waiting for transfers between devices, per_device(): lax.all_gather(span_pair, 'seq', axis=0, tiled=True)  72.9 us
    dot_general x12, matrix products, attend(): jnp.einsum('tkgd,ukd->kgtu', grouped, key_block, preferred_element_type=j...  45.8 us
    dot_general x12, matrix products, attend(): jnp.einsum('kgtu,ukd->kgtd', weights.astype(jnp.bfloat16), value_block, p...  44.2 us
    add x32, other arithmetic, combine(): following[0][:, None, None] * earlier[1] + following[1]  35.5 us
    another operation x2, loops' own time, fold_keys(): running, _ = lax.scan(advance, running, offsets)  24.1 us
    reduce_sum x12, other arithmetic, attend(): weight_sum = weight_sum * shrink + jnp.sum(weights, axis=-1)  10.4 us
  transfers between devices with their start and end apart: 3, of which 1 were waited for; matrix products, arithmetic and copies ran while one was open for 10% of the time, Pallas kernels for 0%

commit v1 on v0

v1 whole, which is shorter than its diff:
```python
import math

import jax
import jax.numpy as jnp
import numpy as np
from jax import lax
from jax.experimental import pallas as pl
from jax.experimental.pallas import tpu as pltpu
from jax.sharding import PartitionSpec as P

MESH = pl.DeviceIdType.MESH
BF = jnp.bfloat16
F32 = jnp.float32
EPS = 1e-06
SCALE = np.float32(1.4426950408889634 / math.sqrt(128.0))
RATES = (10000000.0 ** (-np.arange(32) / 32.0)).astype(np.float32)
NEG = -1e30

T = 128
HEADS = 8
ROWS = HEADS * T
CHUNK = 2048
RB = 256
NX, NZ = 4, 8
GROUPS = 16


def nt_dot(a, b):
    return lax.dot_general(a, b, (((1,), (1,)), ((), ())), preferred_element_type=F32)


def dot(a, b):
    return jnp.dot(a, b, preferred_element_type=F32)


def split2(value):
    high = value.astype(BF)
    return high, (value - high.astype(F32)).astype(BF)


class Copies:
    def __init__(self, send_sem, recv_sem):
        self.send_sem, self.recv_sem = send_sem, recv_sem
        self.made = []

    def make(self, src, dst, to):
        number = len(self.made)
        copy = pltpu.make_async_remote_copy(
            src_ref=src,
            dst_ref=dst,
            send_sem=self.send_sem.at[number],
            recv_sem=self.recv_sem.at[number],
            device_id=to,
            device_id_type=MESH,
        )
        self.made.append(copy)
        return copy

    def start(self, src, dst, to):
        copy = self.make(src, dst, to)
        copy.start()
        return copy

    def finish(self):
        for copy in self.made:
            copy.wait_send()


N_COPIES = 80


def kernel(
    lq_hbm,
    lk_hbm,
    lv_hbm,
    ld_ref,
    gain_ref,
    sq_hbm,
    skv_hbm,
    cache_hbm,
    rates_ref,
    lens_ref,
    start_ref,
    lout_ref,
    att_ref,
    lq,
    lk,
    lv,
    sq,
    skv,
    ks,
    vs,
    within,
    expcol,
    lsend,
    lrecv,
    tsend,
    trecv,
    psend,
    precv,
    ssend,
    srecv,
    qown,
    qpar,
    qhl,
    bias,
    m_ref,
    acc_ref,
    s_buf,
    part_out,
    part_stat,
    part_out_in,
    part_stat_in,
    lsem,
    ssem,
    rsem,
    tssem,
    trsem,
    pssem,
    prsem,
    xsem,
    xrsem,
):
    seq, blk = lax.axis_index("seq"), lax.axis_index("blk")
    x = lax.rem(seq, NX)
    group = seq // NX
    z = lax.rem(group, NZ)
    yh = group // NZ
    yl, core = blk // 2, lax.rem(blk, 2)

    def at(yh_, z_, x_, blk_):
        return ((yh_ * NZ + z_) * NX + x_, blk_)

    def x_peer(d):
        return at(yh, z, lax.rem(x + d, NX), blk)

    def group_of(g):
        return (g * NX + x, blk)

    z_up, z_down = lax.rem(z + 1, NZ), lax.rem(z + NZ - 1, NZ)
    up, down = at(yh, z_up, x, blk), at(yh, z_down, x, blk)
    sibling = blk + 1 - 2 * core
    y_partner = at(1 - yh, z, x, blk)

    loads = [
        pltpu.make_async_copy(src, dst, lsem.at[i])
        for i, (src, dst) in enumerate(
            [
                (skv_hbm, skv),
                (lk_hbm, lk),
                (lv_hbm, lv),
                (lq_hbm, lq),
                (sq_hbm, sq),
                (cache_hbm.at[blk, 0], ks.at[pl.ds(8 + 2 * blk, 2)]),
                (cache_hbm.at[blk, 1], vs.at[pl.ds(8 + 2 * blk, 2)]),
            ]
        )
    ]
    for load in loads:
        load.start()

    barrier = pltpu.get_barrier_semaphore()

    def greet(device):
        pl.semaphore_signal(barrier, inc=1, device_id=device, device_id_type=MESH)

    for d in range(1, NX):
        greet(x_peer(d))
    for d in range(1, GROUPS):
        greet(group_of(lax.rem(group + d, GROUPS)))
    greet((seq, sibling))
    for yh_ in range(2):
        for core_ in range(2):
            greet(at(yh_, z, x, (1 - yl) * 2 + core_))
    pl.semaphore_wait(barrier, 23)

    copies = Copies(ssem, rsem)

    loads[0].wait()
    vs[0, x] = skv[1]
    vz, vx, kz = {}, [], {}

    def send_vz(step):
        up_from, up_to = (9 - step) % 8, 8 - step
        down_from, down_to = step - 1, step
        if step < 4:
            vz["u", step] = copies.start(vs.at[up_from, x], vs.at[up_to, x], up)
            vz["d", step] = copies.start(vs.at[down_from, x], vs.at[down_to, x], down)
        else:
            half = T // 2
            first, last = pl.ds(0, half), pl.ds(half, half)
            vz["u", step] = copies.start(vs.at[up_from, x, first], vs.at[up_to, x, first], up)
            vz["d", step] = copies.start(vs.at[down_from, x, last], vs.at[down_to, x, last], down)

    def wait_vz(step):
        vz["u", step].wait_recv()
        vz["d", step].wait_recv()

    def send_vx(slot):
        for d in range(1, NX):
            vx.append(copies.start(vs.at[slot, x], vs.at[slot, x], x_peer(d)))

    def send_kz(step):
        up_from, up_to = (9 - step) % 8, 8 - step
        down_from, down_to = step - 1, step
        if step < 4:
            kz["u", step] = copies.start(ks.at[up_from], ks.at[up_to], up)
            kz["d", step] = copies.start(ks.at[down_from], ks.at[down_to], down)
        else:
            first, last = pl.ds(0, 2), pl.ds(2, 2)
            kz["u", step] = copies.start(ks.at[up_from, first], ks.at[up_to, first], up)
            kz["d", step] = copies.start(ks.at[down_from, last], ks.at[down_to, last], down)

    def wait_kz(step):
        kz["u", step].wait_recv()
        kz["d", step].wait_recv()

    send_vz(1)
    send_vx(0)

    lane = lax.broadcasted_iota(jnp.int32, (T, T), 1)
    row = lax.broadcasted_iota(jnp.int32, (T, T), 0)
    positions = (start_ref[0] + seq * T + row).astype(F32)
    angles = positions * rates_ref[0:1, :]
    sine = jnp.sin(angles)
    cos_t = jnp.where(lane < 64, jnp.cos(angles), 1.0)
    sin_t = jnp.where(lane < 32, -sine, jnp.where(lane < 64, sine, 0.0))

    def rotate(features):
        partner = jnp.where(lane < 32, pltpu.roll(features, 96, 1), pltpu.roll(features, 32, 1))
        return features * cos_t + partner * sin_t

    ks[0, x] = rotate(skv[0].astype(F32)).astype(BF)
    kx = [copies.start(ks.at[0, x], ks.at[0, x], x_peer(d)) for d in range(1, NX)]

    cumulative = ld_ref[...]
    lane8 = lax.broadcasted_iota(jnp.int32, (HEADS, T), 1)
    shift = 1
    while shift < T:
        cumulative = cumulative + jnp.where(lane8 >= shift, pltpu.roll(cumulative, shift, 1), 0.0)
        shift *= 2
    last = cumulative[:, T - 1 : T]
    tail = jnp.exp(last - cumulative)
    decay_high, decay_low = split2(jnp.broadcast_to(jnp.exp(last), (HEADS, T)))
    loads[1].wait()
    loads[2].wait()
    for h in range(HEADS):
        cols = pl.ds(h * T, T)
        keys_t = lk[:, cols].astype(F32).T * tail[h : h + 1, :]
        local = dot(keys_t.astype(BF), lv[:, cols])
        lsend[h // 2, pl.ds((h % 2) * T, T)] = local.astype(BF)
    for pair in range(NX):
        rows_ = [
            jnp.broadcast_to(part[h : h + 1, :].astype(F32), (8, T))
            for h in (2 * pair, 2 * pair + 1)
            for part in (decay_high, decay_low)
        ]
        lsend[pair, pl.ds(2 * T, 32)] = jnp.concatenate(rows_, axis=0).astype(BF)
    lx = [
        copies.start(lsend.at[lax.rem(x + d, NX)], lrecv.at[x], x_peer(d)) for d in range(1, NX)
    ]
    lrecv[x] = lsend[x]

    cache_in = []
    for kv, buf in ((0, ks), (1, vs)):
        cache_in.append(
            copies.start(
                cache_hbm.at[sibling, kv], buf.at[pl.ds(8 + 2 * blk, 2)], (seq, sibling)
            )
        )
        for flip in range(2):
            for swap in range(2):
                yh_ = yh + flip - 2 * flip * yh
                other = (1 - yl) * 2 + core + swap - 2 * swap * core
                cache_in.append(
                    copies.start(
                        cache_hbm.at[other, kv, yh],
                        buf.at[8 + 2 * blk + yh],
                        at(yh_, z, x, other),
                    )
                )

    causal = row >= lane
    loads[3].wait()
    for h in range(HEADS):
        cols = pl.ds(h * T, T)
        across = jnp.broadcast_to(cumulative[h : h + 1, :], (T, T))
        downward = across.T
        weights = jnp.where(causal, jnp.exp(jnp.minimum(downward - across, 0.0)), 0.0)
        scores = nt_dot(lq[:, cols], lk[:, cols])
        within[h] = dot((scores * weights).astype(BF), lv[:, cols])
        expcol[h] = jnp.exp(downward)

    for copy in kx:
        copy.wait_recv()
    send_kz(1)
    wait_vz(1)
    send_vz(2)
    send_vx(7)
    send_vx(1)

    for copy in lx:
        copy.wait_recv()

    def decay_of(i):
        tile = lrecv[i, pl.ds(2 * T, 32)].astype(F32)
        return [tile[0:8] + tile[8:16], tile[16:24] + tile[24:32]]

    def state_rows(i, k):
        return lrecv[i, pl.ds(k * T, T)].astype(F32)

    decays = [decay_of(i) for i in range(NX)]
    tall = [[jnp.concatenate([d_] * 16, axis=0) for d_ in pair] for pair in decays]
    for k in range(2):
        total, overall = state_rows(0, k), decays[0][k]
        for i in range(1, NX):
            total = total * tall[i][k] + state_rows(i, k)
            overall = overall * decays[i][k]
        high, low = split2(overall)
        tail_rows = jnp.concatenate([high.astype(F32), low.astype(F32)], axis=0).astype(BF)
        for i in range(8):
            tsend[8 * k + i, pl.ds(0, 16)] = total[16 * i : 16 * i + 16].astype(BF)
            tsend[8 * k + i, pl.ds(16, 16)] = tail_rows

    def t_copy(d):
        to = lax.rem(group + d, GROUPS)
        return pltpu.make_async_remote_copy(
            src_ref=tsend.at[to],
            dst_ref=trecv.at[group],
            send_sem=tssem.at[d],
            recv_sem=trsem.at[d],
            device_id=group_of(to),
            device_id_type=MESH,
        )

    def p_copy(d):
        to = lax.rem(group + d, GROUPS)
        return pltpu.make_async_remote_copy(
            src_ref=psend.at[to],
            dst_ref=precv.at[group],
            send_sem=pssem.at[d],
            recv_sem=prsem.at[d],
            device_id=group_of(to),
            device_id_type=MESH,
        )

    def each_group(action):
        def one(d, carry):
            action(d)
            return carry

        lax.fori_loop(1, GROUPS, one, 0)

    each_group(lambda d: t_copy(d).start())
    trecv[group] = tsend[group]

    wait_kz(1)
    send_kz(2)
    wait_vz(2)
    send_vz(3)
    send_vx(6)
    send_vx(2)

    each_group(lambda d: t_copy(d).wait_recv())
    state = jnp.zeros((16, T), F32)
    for g in range(GROUPS):
        psend[g] = state.astype(BF)
        if g < GROUPS - 1:
            tile = trecv[g, pl.ds(16, 16)].astype(F32)
            decay = tile[0:8] + tile[8:16]
            state = state * jnp.concatenate([decay, decay], axis=0) + trecv[
                g, pl.ds(0, 16)
            ].astype(F32)
    each_group(lambda d: p_copy(d).start())
    precv[group] = psend[group]

    wait_kz(2)
    send_kz(3)
    wait_vz(3)
    send_vz(4)
    send_vx(5)
    send_vx(3)

    each_group(lambda d: p_copy(d).wait_recv())
    for k in range(2):
        state = precv[pl.ds(8 * k, 8)].astype(F32).reshape(T, T)
        for i in range(NX):
            ssend[i, pl.ds(k * T, T)] = state.astype(BF)
            if i < NX - 1:
                state = state * tall[i][k] + state_rows(i, k)
    sx = [
        copies.start(ssend.at[lax.rem(x + d, NX)], srecv.at[x], x_peer(d)) for d in range(1, NX)
    ]
    srecv[x] = ssend[x]

    wait_kz(3)
    send_kz(4)
    wait_vz(4)
    send_vx(4)

    col = lax.broadcasted_iota(jnp.int32, (8, CHUNK), 1)
    visible_from = 512 * (8 - z)
    bias[0] = jnp.where((col < x * T) | (col >= visible_from), 0.0, NEG)
    bias[1] = jnp.where(col + CHUNK >= visible_from, 0.0, NEG)
    for c in range(2):
        bias[2 + c] = jnp.where(
            ((col < 1024) & (col < lens_ref[2 * c]))
            | ((col >= 1024) & (col - 1024 < lens_ref[2 * c + 1])),
            0.0,
            NEG,
        )
    bias[4] = jnp.zeros((8, CHUNK), F32)

    loads[4].wait()
    for copy in sx:
        copy.wait_recv()
    for h in range(HEADS):
        cols = pl.ds(h * T, T)
        carried = dot(lq[:, cols], srecv[h // 2, pl.ds((h % 2) * T, T)])
        light = within[h] + expcol[h] * carried
        mean = jnp.mean(light * light, axis=1, keepdims=True)
        out = (light * lax.rsqrt(mean + EPS) * gain_ref[h : h + 1, :]).astype(BF)
        lout_ref[:, cols] = out
        query = rotate(sq[:, cols].astype(F32) + out.astype(F32)).astype(BF)
        rows_ = pl.ds(h * T, T)
        qown[rows_, :] = query
        high, low = split2(query.astype(F32) * SCALE)
        qhl[0, rows_, pl.ds(0, T)] = high
        qhl[0, rows_, pl.ds(T, T)] = low

    def q_copy():
        return pltpu.make_async_remote_copy(
            src_ref=qown,
            dst_ref=qpar,
            send_sem=xsem.at[0],
            recv_sem=xrsem.at[0],
            device_id=y_partner,
            device_id_type=MESH,
        )

    def back_copies():
        return [
            pltpu.make_async_remote_copy(
                src_ref=src,
                dst_ref=dst,
                send_sem=xsem.at[1 + i],
                recv_sem=xrsem.at[1 + i],
                device_id=y_partner,
                device_id_type=MESH,
            )
            for i, (src, dst) in enumerate(
                [(part_out, part_out_in), (part_stat, part_stat_in)]
            )
        ]

    @pl.when(yh == 1)
    def _():
        q_copy().start()

    own_k, own_v = ks[0, x], vs[0, x]
    own_k2 = jnp.concatenate([own_k, own_k], axis=1)
    own_v2 = jnp.concatenate([own_v, jnp.ones_like(own_v)], axis=1)
    for h in range(HEADS):
        rows_ = pl.ds(h * T, T)
        scores = jnp.where(causal, nt_dot(qhl[0, rows_, :], own_k2), NEG)
        peak = jnp.broadcast_to(jnp.max(scores, axis=1, keepdims=True), (T, T))
        m_ref[0, rows_, :] = peak
        acc_ref[0, rows_, :] = dot(jnp.exp2(scores - peak).astype(BF), own_v2)

    @pl.when(yh == 0)
    def _():
        m_ref[1] = jnp.full((ROWS, T), NEG, F32)
        acc_ref[1] = jnp.zeros((ROWS, 2 * T), F32)

    wait_kz(4)
    for copy in vx + cache_in:
        copy.wait_recv()
    loads[5].wait()
    loads[6].wait()

    def finish_rows(which, h):
        rows_ = pl.ds(h * T, T)
        return m_ref[which, rows_, :], acc_ref[which, rows_, 0:T], acc_ref[which, rows_, T : 2 * T]

    def job(j, carry):
        early = 1 - yh
        which = early * lax.rem(j // 2, 2)
        chunk = early * (lax.rem(j, 2) + 2 * (j // 4)) + yh * j
        mask = chunk + which * (4 - chunk)

        @pl.when((yh == 0) & (j == 2))
        def _():
            q_copy().wait_recv()
            high, low = split2(qpar[...].astype(F32) * SCALE)
            qhl[1, :, pl.ds(0, T)] = high
            qhl[1, :, pl.ds(T, T)] = low

        keys = ks[pl.ds(4 * chunk, 4)].reshape(CHUNK, T)
        keys2 = jnp.concatenate([keys, keys], axis=1)
        values = vs[pl.ds(4 * chunk, 4)].reshape(CHUNK, T)
        values2 = jnp.concatenate([values, jnp.ones_like(values)], axis=1)
        shade = bias[mask, 0:1, :]
        steps = ROWS // RB
        s_buf[0] = nt_dot(qhl[which, pl.ds(0, RB), :], keys2)
        for r in range(steps):
            rows_ = pl.ds(r * RB, RB)
            if r < steps - 1:
                s_buf[(r + 1) % 2] = nt_dot(qhl[which, pl.ds((r + 1) * RB, RB), :], keys2)
            scores = s_buf[r % 2] + shade
            best = scores[:, 0:T]
            for i in range(1, CHUNK // T):
                best = jnp.maximum(best, scores[:, i * T : (i + 1) * T])
            old = m_ref[which, rows_, :]
            new = jnp.maximum(old, jnp.max(best, axis=1, keepdims=True))
            shrink = jnp.exp2(old - new)
            m_ref[which, rows_, :] = new
            weights = jnp.exp2(scores - jnp.concatenate([new] * (CHUNK // T), axis=1)).astype(BF)
            acc_ref[which, rows_, :] = acc_ref[which, rows_, :] * jnp.concatenate(
                [shrink, shrink], axis=1
            ) + dot(weights, values2)

        @pl.when((yh == 0) & (j == 3))
        def _():
            for h in range(HEADS):
                peak, top, total = finish_rows(1, h)
                part_out[pl.ds(h * T, T), :] = (top / total).astype(BF)
                part_stat[pl.ds(h, 1), :] = (peak + jnp.log2(total)).T[0:1, :]
            for copy in back_copies():
                copy.start()

        return carry

    lax.fori_loop(0, 6 - 2 * yh, job, 0)

    @pl.when(yh == 0)
    def _():
        for h in range(HEADS):
            _, top, total = finish_rows(0, h)
            att_ref[:, pl.ds(h * T, T)] = (top / total).astype(BF)
        for copy in back_copies():
            copy.wait_send()

    @pl.when(yh == 1)
    def _():
        q_copy().wait_send()
        for copy in back_copies():
            copy.wait_recv()
        for h in range(HEADS):
            peak, top, total = finish_rows(0, h)
            other = jnp.broadcast_to(part_stat_in[pl.ds(h, 1), :], (T, T)).T
            best = jnp.maximum(peak, other)
            mine, theirs = jnp.exp2(peak - best), jnp.exp2(other - best)
            merged = top * mine + part_out_in[pl.ds(h * T, T), :].astype(F32) * theirs
            att_ref[:, pl.ds(h * T, T)] = (merged / (total * mine + theirs)).astype(BF)

    each_group(lambda d: t_copy(d).wait_send())
    each_group(lambda d: p_copy(d).wait_send())
    copies.finish()


def per_device(lq, lk, lv, ld, gain, sq, skv, cache, lens, start):
    any_space = pl.BlockSpec(memory_space=pl.ANY)
    vmem = pl.BlockSpec(memory_space=pltpu.VMEM)
    smem = pl.BlockSpec(memory_space=pltpu.SMEM)
    rates = np.zeros((8, T), np.float32)
    rates[:, 0:32] = RATES
    rates[:, 32:64] = RATES
    skv_t = skv.reshape(T, 2, T).transpose(1, 0, 2)
    cache_t = cache.transpose(2, 1, 0, 3).reshape(4, 2, 2, NX, T, T)
    scratch = [
        pltpu.VMEM((T, ROWS), BF),
        pltpu.VMEM((T, ROWS), BF),
        pltpu.VMEM((T, ROWS), BF),
        pltpu.VMEM((T, ROWS), BF),
        pltpu.VMEM((2, T, T), BF),
        pltpu.VMEM((16, NX, T, T), BF),
        pltpu.VMEM((16, NX, T, T), BF),
        pltpu.VMEM((HEADS, T, T), F32),
        pltpu.VMEM((HEADS, T, T), F32),
        pltpu.VMEM((NX, 2 * T + 32, T), BF),
        pltpu.VMEM((NX, 2 * T + 32, T), BF),
        pltpu.VMEM((GROUPS, 32, T), BF),
        pltpu.VMEM((GROUPS, 32, T), BF),
        pltpu.VMEM((GROUPS, 16, T), BF),
        pltpu.VMEM((GROUPS, 16, T), BF),
        pltpu.VMEM((NX, 2 * T, T), BF),
        pltpu.VMEM((NX, 2 * T, T), BF),
        pltpu.VMEM((ROWS, T), BF),
        pltpu.VMEM((ROWS, T), BF),
        pltpu.VMEM((2, ROWS, 2 * T), BF),
        pltpu.VMEM((5, 8, CHUNK), F32),
        pltpu.VMEM((2, ROWS, T), F32),
        pltpu.VMEM((2, ROWS, 2 * T), F32),
        pltpu.VMEM((2, RB, CHUNK), F32),
        pltpu.VMEM((ROWS, T), BF),
        pltpu.VMEM((HEADS, T), F32),
        pltpu.VMEM((ROWS, T), BF),
        pltpu.VMEM((HEADS, T), F32),
        pltpu.SemaphoreType.DMA((7,)),
        pltpu.SemaphoreType.DMA((N_COPIES,)),
        pltpu.SemaphoreType.DMA((N_COPIES,)),
        pltpu.SemaphoreType.DMA((GROUPS,)),
        pltpu.SemaphoreType.DMA((GROUPS,)),
        pltpu.SemaphoreType.DMA((GROUPS,)),
        pltpu.SemaphoreType.DMA((GROUPS,)),
        pltpu.SemaphoreType.DMA((3,)),
        pltpu.SemaphoreType.DMA((3,)),
    ]
    return pl.pallas_call(
        kernel,
        out_shape=(
            jax.ShapeDtypeStruct((T, ROWS), BF),
            jax.ShapeDtypeStruct((T, ROWS), BF),
        ),
        in_specs=[
            any_space,
            any_space,
            any_space,
            vmem,
            vmem,
            any_space,
            any_space,
            any_space,
            vmem,
            smem,
            smem,
        ],
        out_specs=(vmem, vmem),
        scratch_shapes=scratch,
        compiler_params=pltpu.CompilerParams(
            collective_id=0, has_side_effects=True, vmem_limit_bytes=48 * 2**20
        ),
    )(lq, lk, lv, ld, gain.reshape(HEADS, T), sq, skv_t, cache_t, jnp.asarray(rates), lens, start)


def solution(mesh):
    in_specs = (
        P("seq", "blk"),
        P("seq", "blk"),
        P("seq", "blk"),
        P("blk", "seq"),
        P("blk"),
        P("seq", "blk"),
        P("seq", None, "blk", None),
        P("blk", None, None, None),
        P(),
        P(),
    )
    out_specs = (P("seq", "blk"), P("seq", "blk"))
    return jax.shard_map(
        per_device, mesh=mesh, in_specs=in_specs, out_specs=out_specs, check_vma=False
    )
```

time: 483 us -> 67.4 us (0.14)
  blocking collectives: 187 us -> 0 us
  matrix products: 94.3 us -> 0 us
  waiting for transfers between devices: 72.9 us -> 0 us
  other arithmetic: 62.3 us -> 0 us
  Pallas kernels: 0 us -> 61.2 us
  loops' own time: 25.4 us -> 0 us
  between operations: 15.7 us -> 1.42 us
  local copies, waits for them, and re-layouts: 17.6 us -> 4.24 us
    unnamed x1 -> x0, blocking collectives: 187 us -> none
    dot_general x28 -> x0, matrix products: 94.3 us -> none  [the longest x12 45.8 us: attend(): jnp.einsum('tkgd,ukd->kgtu', grouped, key_block, preferred_element_type=j...]
    all_gather x2 -> x0, waiting for transfers between devices: 72.9 us -> none  [the longest x1 72.9 us: per_device(): lax.all_gather(span_pair, 'seq', axis=0, tiled=True)]
    pallas_call x0 -> x1, Pallas kernels: none -> 61.2 us  [per_device(): pl.pallas_call(kernel, out_shape=(jax.ShapeDtypeStruct((T, ROWS), BF), ja...]
    add x61 -> x0, other arithmetic: 40.9 us -> none  [the longest x32 35.5 us: combine(): following[0][:, None, None] * earlier[1] + following[1]]
    another operation x3 -> x0, loops' own time: 25.4 us -> none  [the longest x2 24.1 us: fold_keys(): running, _ = lax.scan(advance, running, offsets)]
    reduce_sum x16 -> x0, other arithmetic: 10.7 us -> none  [the longest x12 10.4 us: attend(): weight_sum = weight_sum * shrink + jnp.sum(weights, axis=-1)]
    dynamic_slice x12 -> x0, local copies, waits for them, and re-layouts: 7.03 us -> none  [fold_keys(): running, _ = lax.scan(advance, running, offsets)]
  transfers between devices with their start and end apart: 3 -> 0, of which waited for: 1 -> 0; matrix products, arithmetic and copies ran while one was open for 10% -> 0% of each run, Pallas kernels for 0% -> 0%
where the time goes in v1:
time: 67.4 us; the launch traced here: 66.9 us
  Pallas kernels  61.2 us (91%)
  local copies, waits for them, and re-layouts  4.24 us (6%)
  between operations  1.42 us (2%)
    pallas_call x1, Pallas kernels, per_device(): pl.pallas_call(kernel, out_shape=(jax.ShapeDtypeStruct((T, ROWS), BF), ja...  61.2 us
    unnamed x19, local copies, waits for them, and re-layouts  2.31 us
    transpose x1, local copies, waits for them, and re-layouts, per_device(): cache_t = cache.transpose(2, 1, 0, 3).reshape(4, 2, 2, NX, T, T)  1.94 us

profile of v1, /device:TPU:16, one launch (start us, length us, event | category | flops | bytes accessed | tf_op | source)
XLA Modules:
  0.0 66.9 jit_solution(14461009841800745690)
XLA Ops:
  1.3 0.9 %copy.16 = bf16[128,2,1,128]{3,0,1,2:T(8,128)(2,1)S(1)} copy(bf16[128,2,1,128]{3,1,2,0:T(2,128)(2,1)} %param.17) | data formatting | bytes 131072 | tf_op args[6]
  2.1 0.0 copy-start
  2.1 0.0 copy-start.1
  2.2 0.0 copy-start.2
  2.2 0.0 copy-start.3
  2.2 0.0 copy-start.4
  2.2 0.0 copy-start.5
  2.2 0.0 copy-start.6
  2.2 0.0 copy-start.7
  2.2 1.9 %copy.14 = bf16[4,2,1024,128]{3,2,1,0:T(8,128)(2,1)S(1)} copy(bf16[4,2,1024,128]{3,0,1,2:T(4,128)(2,1)} %bitcast.11) | data formatting | bytes 4194304 | tf_op jit(solution)/shard_map/transpose | solution.py:569
  4.2 0.0 copy-done
  4.2 0.0 copy-done.1
  4.2 0.0 copy-done.2
  4.2 0.0 copy-done.3
  4.2 0.0 copy-done.4
  4.2 0.0 copy-done.5
  4.2 0.0 copy-done.6
  4.2 0.0 copy-done.7
  4.2 61.2 %shard_map.122 = (bf16[128,1024]{1,0:T(8,128)(2,1)S(1)}, bf16[128,1024]{1,0:T(8,128)(2,1)S(1)}) custom-call(bf16[128,1024]{1,0:T(8,128)(2,1)S(1)} %copy-done, bf16[128,1024]{1,0:T(8,128)(2,1)S(1)} %copy-done.1, bf16[128,1024]{1,0:T(8,128)(2,1)S(1)} %copy-done.2, f32[8,128]{1,0:T(8,128)S(1)} %copy-done.4, f32[8,128]{1,0:T(8,128)S(1)} %bitcast.10, ...), custom_call_target="tpu_custom_call" | custom-call | tf_op jit(solution)/shard_map/pallas_call | solution.py:609
  65.5 0.7 %copy.20 = bf16[128,1024]{1,0:T(8,128)(2,1)} copy(bf16[128,1024]{1,0:T(8,128)(2,1)S(1)} %get-tuple-element.4) | data formatting | bytes 524288
  66.2 0.7 %copy.21 = bf16[128,1024]{1,0:T(8,128)(2,1)} copy(bf16[128,1024]{1,0:T(8,128)(2,1)S(1)} %get-tuple-element.5) | data formatting | bytes 524288
Async XLA Ops:
  2.1 2.0 %copy-start = (bf16[128,1024]{1,0:T(8,128)(2,1)S(1)}, bf16[128,1024]{1,0:T(8,128)(2,1)}, u32[]{:S(2)}) copy-start(bf16[128,1024]{1,0:T(8,128)(2,1)} %lq_hbm.1) | copy-start | bytes 786436
  2.1 2.0 %copy-start.1 = (bf16[128,1024]{1,0:T(8,128)(2,1)S(1)}, bf16[128,1024]{1,0:T(8,128)(2,1)}, u32[]{:S(2)}) copy-start(bf16[128,1024]{1,0:T(8,128)(2,1)} %lk_hbm.1) | copy-start | bytes 786436
  2.2 2.0 %copy-start.2 = (bf16[128,1024]{1,0:T(8,128)(2,1)S(1)}, bf16[128,1024]{1,0:T(8,128)(2,1)}, u32[]{:S(2)}) copy-start(bf16[128,1024]{1,0:T(8,128)(2,1)} %lv_hbm.1) | copy-start | bytes 786436
  2.2 2.0 %copy-start.3 = (bf16[128,1024]{1,0:T(8,128)(2,1)S(1)}, bf16[128,1024]{1,0:T(8,128)(2,1)}, u32[]{:S(2)}) copy-start(bf16[128,1024]{1,0:T(8,128)(2,1)} %sq_hbm.1) | copy-start | bytes 786436
  2.2 2.0 %copy-start.4 = (f32[8,128]{1,0:T(8,128)S(1)}, f32[8,128]{1,0:T(8,128)}, u32[]{:S(2)}) copy-start(f32[8,128]{1,0:T(8,128)} %ld_ref.1) | copy-start | bytes 12292
  2.2 2.0 %copy-start.5 = (f32[1024]{0:T(1024)S(1)}, f32[1024]{0:T(1024)}, u32[]{:S(2)}) copy-start(f32[1024]{0:T(1024)} %param.15) | copy-start | bytes 12292
  2.2 2.0 %copy-start.6 = (f32[8,128]{1,0:T(8,128)S(1)}, f32[8,128]{1,0:T(8,128)}, u32[]{:S(2)}) copy-start(f32[8,128]{1,0:T(8,128)} %constant.2.clone.rates_ref) | copy-start | bytes 12292
  2.2 2.0 %copy-start.7 = (s32[4]{0:T(128)S(1)}, s32[4]{0:T(128)}, u32[]{:S(2)}) copy-start(s32[4]{0:T(128)} %lens_ref.1) | copy-start | bytes 52

commit v2 on v1

v2 whole, which is shorter than its diff:
```python
import math

import jax
import jax.numpy as jnp
import numpy as np
from jax import lax
from jax.experimental import pallas as pl
from jax.experimental.pallas import tpu as pltpu
from jax.sharding import PartitionSpec as P

MESH = pl.DeviceIdType.MESH
BF = jnp.bfloat16
F32 = jnp.float32
EPS = 1e-06
SCALE = np.float32(1.4426950408889634 / math.sqrt(128.0))
RATES = (10000000.0 ** (-np.arange(32) / 32.0)).astype(np.float32)
NEG = -1e30

T = 128
HEADS = 8
ROWS = HEADS * T
CHUNK = 2048
RB = 256
NX, NZ = 4, 8
QZ = 4
SLICE = 2 * T // QZ
GROUPS = 16


def nt_dot(a, b):
    return lax.dot_general(a, b, (((1,), (1,)), ((), ())), preferred_element_type=F32)


def dot(a, b):
    return jnp.dot(a, b, preferred_element_type=F32)


def split2(value):
    high = value.astype(BF)
    return high, (value - high.astype(F32)).astype(BF)


class Copies:
    def __init__(self, send_sem, recv_sem):
        self.send_sem, self.recv_sem = send_sem, recv_sem
        self.made = []

    def make(self, src, dst, to):
        number = len(self.made)
        copy = pltpu.make_async_remote_copy(
            src_ref=src,
            dst_ref=dst,
            send_sem=self.send_sem.at[number],
            recv_sem=self.recv_sem.at[number],
            device_id=to,
            device_id_type=MESH,
        )
        self.made.append(copy)
        return copy

    def start(self, src, dst, to):
        copy = self.make(src, dst, to)
        copy.start()
        return copy

    def finish(self):
        for copy in self.made:
            copy.wait_send()


N_COPIES = 64


def one_hot(major, minor):
    size = major * minor
    out = lax.broadcasted_iota(jnp.int32, (size, size), 0)
    source = lax.broadcasted_iota(jnp.int32, (size, size), 1)
    wanted = lax.rem(out, minor) * major + out // minor
    return jnp.where(source == wanted, 1.0, 0.0).astype(BF)


def kernel(
    lq_hbm,
    lk_hbm,
    lv_hbm,
    ld_ref,
    gain_ref,
    sq_hbm,
    skv_ref,
    cache_hbm,
    rates_ref,
    lens_ref,
    start_ref,
    lout_ref,
    att_ref,
    lq,
    lk,
    lv,
    sq,
    cache_raw,
    cache,
    ks,
    vs,
    within,
    expcol,
    lsend,
    lrecv,
    tsend,
    trecv,
    psend,
    precv,
    ssend,
    srecv,
    qown,
    qpar,
    qhl,
    bias,
    m_ref,
    acc_ref,
    s_buf,
    part_out,
    part_stat,
    part_out_in,
    part_stat_in,
    lsem,
    ssem,
    rsem,
    tssem,
    trsem,
    pssem,
    prsem,
    xsem,
    xrsem,
    ready,
):
    seq, blk = lax.axis_index("seq"), lax.axis_index("blk")
    x = lax.rem(seq, NX)
    z = lax.rem(seq // NX, NZ)
    yh = seq // (NX * NZ)
    yl, core = blk // 2, lax.rem(blk, 2)

    def at(yh_, z_, x_, blk_):
        return ((yh_ * NZ + z_) * NX + x_, blk_)

    def x_peer(d):
        return at(yh, z, lax.rem(x + d, NX), blk)

    group = yh * NZ + z
    quarter, zq = group // QZ, lax.rem(z, QZ)
    first_group = quarter * QZ

    def quarter_peer(d):
        place = lax.rem(zq * NX + x + d, QZ * NX)
        return place // NX, at(0, first_group + place // NX, lax.rem(place, NX), blk)

    def column(g):
        return at(0, g, x, blk)

    up, down = at(yh, lax.rem(z + 1, NZ), x, blk), at(yh, lax.rem(z + NZ - 1, NZ), x, blk)
    sibling = blk + 1 - 2 * core
    y_partner = at(1 - yh, z, x, blk)

    def each(first, last, action):
        def one(d, carry):
            action(d)
            return carry

        lax.fori_loop(first, last, one, 0)

    barrier = pltpu.get_barrier_semaphore()

    def greet(device):
        pl.semaphore_signal(barrier, inc=1, device_id=device, device_id_type=MESH)

    each(1, QZ * NX, lambda d: greet(quarter_peer(d)[1]))
    greet((seq, sibling))
    for yh_ in range(2):
        for core_ in range(2):
            greet(at(yh_, z, x, (1 - yl) * 2 + core_))
    each(first_group + QZ, GROUPS, lambda g: greet(column(g)))

    loads = [
        pltpu.make_async_copy(src, dst, lsem.at[i])
        for i, (src, dst) in enumerate(
            [(lk_hbm, lk), (lv_hbm, lv), (lq_hbm, lq), (sq_hbm, sq), (cache_hbm, cache_raw)]
        )
    ]
    for load in loads:
        load.start()

    cumulative = ld_ref[...]
    lane8 = lax.broadcasted_iota(jnp.int32, (HEADS, T), 1)
    shift = 1
    while shift < T:
        cumulative = cumulative + jnp.where(lane8 >= shift, pltpu.roll(cumulative, shift, 1), 0.0)
        shift *= 2
    last = cumulative[:, T - 1 : T]
    tail = jnp.exp(last - cumulative)
    decay_high, decay_low = split2(jnp.broadcast_to(jnp.exp(last), (HEADS, T)))
    loads[0].wait()
    loads[1].wait()
    for h in range(HEADS):
        cols = pl.ds(h * T, T)
        keys_t = lk[:, cols].astype(F32).T * tail[h : h + 1, :]
        local = dot(keys_t.astype(BF), lv[:, cols])
        lsend[h // 2, pl.ds((h % 2) * T, T)] = local.astype(BF)
    for pair in range(NX):
        rows_ = [
            jnp.broadcast_to(part[h : h + 1, :].astype(F32), (8, T))
            for h in (2 * pair, 2 * pair + 1)
            for part in (decay_high, decay_low)
        ]
        lsend[pair, pl.ds(2 * T, 32)] = jnp.concatenate(rows_, axis=0).astype(BF)
    lrecv[x] = lsend[x]

    lane = lax.broadcasted_iota(jnp.int32, (T, T), 1)
    row = lax.broadcasted_iota(jnp.int32, (T, T), 0)
    positions = (start_ref[0] + seq * T + row).astype(F32)
    angles = positions * rates_ref[0:1, :]
    sine = jnp.sin(angles)
    cos_t = jnp.where(lane < 64, jnp.cos(angles), 1.0)
    sin_t = jnp.where(lane < 32, -sine, jnp.where(lane < 64, sine, 0.0))

    def rotate(features):
        partner = jnp.where(lane < 32, pltpu.roll(features, 96, 1), pltpu.roll(features, 32, 1))
        return features * cos_t + partner * sin_t

    span = dot(one_hot(2, T), skv_ref[...])
    ks[0, x] = rotate(span[0:T]).astype(BF)
    vs[0, x] = span[T : 2 * T].astype(BF)

    pl.semaphore_wait(barrier, QZ * NX - 1 + 5 + first_group)
    each(
        0,
        first_group,
        lambda g: pl.semaphore_signal(ready, inc=1, device_id=column(g), device_id_type=MESH),
    )

    copies = Copies(ssem, rsem)
    lx = [
        copies.start(lsend.at[lax.rem(x + d, NX)], lrecv.at[x], x_peer(d)) for d in range(1, NX)
    ]

    vz, vx, kz = {}, [], {}

    def send_vz(step):
        if step < 4:
            vz["u", step] = copies.start(vs.at[step - 1, x], vs.at[step, x], up)
            vz["d", step] = copies.start(vs.at[(9 - step) % 8, x], vs.at[8 - step, x], down)
        else:
            first, last_ = pl.ds(0, T // 2), pl.ds(T // 2, T // 2)
            vz["u", step] = copies.start(vs.at[3, x, first], vs.at[4, x, first], up)
            vz["d", step] = copies.start(vs.at[5, x, last_], vs.at[4, x, last_], down)

    def wait_vz(step):
        vz["u", step].wait_recv()
        vz["d", step].wait_recv()

    def send_vx(slot):
        for d in range(1, NX):
            vx.append(copies.start(vs.at[slot, x], vs.at[slot, x], x_peer(d)))

    def send_kz(step):
        if step < 4:
            kz["u", step] = copies.start(ks.at[step - 1], ks.at[step], up)
            kz["d", step] = copies.start(ks.at[(9 - step) % 8], ks.at[8 - step], down)
        else:
            first, last_ = pl.ds(0, 2), pl.ds(2, 2)
            kz["u", step] = copies.start(ks.at[3, first], ks.at[4, first], up)
            kz["d", step] = copies.start(ks.at[5, last_], ks.at[4, last_], down)

    def wait_kz(step):
        kz["u", step].wait_recv()
        kz["d", step].wait_recv()

    kx = [copies.start(ks.at[0, x], ks.at[0, x], x_peer(d)) for d in range(1, NX)]

    causal = row >= lane
    loads[2].wait()
    for h in range(HEADS):
        cols = pl.ds(h * T, T)
        across = jnp.broadcast_to(cumulative[h : h + 1, :], (T, T))
        downward = across.T
        weights = jnp.where(causal, jnp.exp(jnp.minimum(downward - across, 0.0)), 0.0)
        scores = nt_dot(lq[:, cols], lk[:, cols])
        within[h] = dot((scores * weights).astype(BF), lv[:, cols])
        expcol[h] = jnp.exp(downward)

    for copy in lx:
        copy.wait_recv()

    def decay_of(tile):
        wide = tile.astype(F32)
        return [wide[0:8] + wide[8:16], wide[16:24] + wide[24:32]]

    def tall(decay, rows_):
        return jnp.concatenate([decay] * (rows_ // 8), axis=0)

    def two_parts(decay):
        high, low = split2(decay)
        return [high.astype(F32), low.astype(F32)]

    decays = [decay_of(lrecv[i, pl.ds(2 * T, 32)]) for i in range(NX)]
    ones8 = jnp.ones((8, T), F32)
    overall = [ones8, ones8]
    totals = [jnp.zeros((T, T), F32)] * 2
    for i in range(NX):
        for k in range(2):
            ssend[i, pl.ds(k * T, T)] = totals[k].astype(BF)
            totals[k] = totals[k] * tall(decays[i][k], T) + lrecv[i, pl.ds(k * T, T)].astype(F32)
        ssend[i, pl.ds(2 * T, 32)] = jnp.concatenate(
            two_parts(overall[0]) + two_parts(overall[1]), axis=0
        ).astype(BF)
        overall = [overall[k] * decays[i][k] for k in range(2)]
    for k in range(2):
        tail_rows = jnp.concatenate(two_parts(overall[k]), axis=0).astype(BF)
        for i in range(QZ // 2):
            piece = totals[k][SLICE * i : SLICE * (i + 1)]
            tsend[QZ // 2 * k + i, pl.ds(0, SLICE)] = piece.astype(BF)
            tsend[QZ // 2 * k + i, pl.ds(SLICE, 16)] = tail_rows

    def t_copy(g):
        return pltpu.make_async_remote_copy(
            src_ref=tsend.at[lax.rem(g, QZ)],
            dst_ref=trecv.at[group],
            send_sem=tssem.at[g],
            recv_sem=trsem.at[group],
            device_id=column(g),
            device_id_type=MESH,
        )

    def t_arrival(g):
        return pltpu.make_async_remote_copy(
            src_ref=tsend.at[0],
            dst_ref=trecv.at[g],
            send_sem=tssem.at[g],
            recv_sem=trsem.at[g],
            device_id=column(g),
            device_id_type=MESH,
        )

    def quarter_group(d):
        return first_group + lax.rem(zq + d, QZ)

    each(1, QZ, lambda d: t_copy(quarter_group(d)).start())
    trecv[group] = tsend[zq]
    sx = [
        copies.start(ssend.at[lax.rem(x + d, NX)], srecv.at[x], x_peer(d)) for d in range(1, NX)
    ]
    srecv[x] = ssend[x]

    @pl.when(quarter < 3)
    def _():
        pl.semaphore_wait(ready, GROUPS - QZ - first_group)

    each(first_group + QZ, GROUPS, lambda g: t_copy(g).start())
    send_vz(1)
    send_vx(0)
    for copy in kx:
        copy.wait_recv()
    send_kz(1)

    loads[4].wait()
    sort = one_hot(8, 32)

    def relayout(b, carry):
        part = dot(sort, cache_raw[pl.ds(pl.multiple_of(b * 256, 256), 256), :]).astype(BF)
        rows_ = pl.ds(pl.multiple_of(lax.rem(b, 4) * 32, 32), 32)
        for kv in range(2):
            for h in range(4):
                at_ = (kv * 4 + h) * 32
                cache[h, kv, b // 16, lax.rem(b // 4, 4), rows_] = part[at_ : at_ + 32]
        return carry

    lax.fori_loop(0, 32, relayout, 0, unroll=4)

    cache_in = []
    for kv, buf in ((0, ks), (1, vs)):
        cache_in.append(
            copies.start(cache.at[sibling, kv], buf.at[pl.ds(8 + 2 * blk, 2)], (seq, sibling))
        )
        for flip in range(2):
            for swap in range(2):
                yh_ = yh + flip - 2 * flip * yh
                other = (1 - yl) * 2 + core + swap - 2 * swap * core
                cache_in.append(
                    copies.start(
                        cache.at[other, kv, yh],
                        buf.at[8 + 2 * blk + yh],
                        at(yh_, z, x, other),
                    )
                )
        buf[pl.ds(8 + 2 * blk, 2)] = cache[blk, kv]

    wait_vz(1)
    send_vz(2)
    wait_kz(1)
    send_kz(2)

    def chain(g, state):
        tile = trecv[g, pl.ds(SLICE, 16)].astype(F32)
        return state * tall(tile[0:8] + tile[8:16], SLICE) + trecv[g, pl.ds(0, SLICE)].astype(F32)

    def earlier(g, state):
        t_arrival(g).wait_recv()
        return chain(g, state)

    each(1, QZ, lambda d: t_arrival(quarter_group(d)).wait_recv())
    state = lax.fori_loop(0, first_group, earlier, jnp.zeros((SLICE, T), F32))
    for i in range(QZ):
        psend[i] = state.astype(BF)
        if i < QZ - 1:
            state = chain(first_group + i, state)

    def p_copy(d):
        z_, device = quarter_peer(d)
        return pltpu.make_async_remote_copy(
            src_ref=psend.at[z_],
            dst_ref=precv.at[x, zq],
            send_sem=pssem.at[d],
            recv_sem=prsem.at[d],
            device_id=device,
            device_id_type=MESH,
        )

    each(1, QZ * NX, lambda d: p_copy(d).start())
    precv[x, zq] = psend[zq]

    wait_vz(2)
    send_vz(3)
    send_vx(1)
    send_vx(7)
    wait_kz(2)
    send_kz(3)

    col = lax.broadcasted_iota(jnp.int32, (8, CHUNK), 1)
    visible_to = 512 * (z + 1)
    bias[0] = jnp.where((col < x * T) | ((col >= 512) & (col < visible_to)), 0.0, NEG)
    bias[1] = jnp.where(col + CHUNK < visible_to, 0.0, NEG)
    for c in range(2):
        bias[2 + c] = jnp.where(
            ((col < 1024) & (col < lens_ref[2 * c]))
            | ((col >= 1024) & (col - 1024 < lens_ref[2 * c + 1])),
            0.0,
            NEG,
        )
    bias[4] = jnp.zeros((8, CHUNK), F32)

    wait_vz(3)
    send_vz(4)
    send_vx(2)
    send_vx(6)

    for copy in sx:
        copy.wait_recv()
    loads[3].wait()
    each(1, QZ * NX, lambda d: p_copy(d).wait_recv())

    def q_copy(h):
        rows_ = pl.ds(h * T, T)
        return pltpu.make_async_remote_copy(
            src_ref=qown.at[rows_],
            dst_ref=qpar.at[rows_],
            send_sem=xsem.at[2 + h],
            recv_sem=xrsem.at[2 + h],
            device_id=y_partner,
            device_id_type=MESH,
        )

    def back_copies():
        return [
            pltpu.make_async_remote_copy(
                src_ref=src,
                dst_ref=dst,
                send_sem=xsem.at[i],
                recv_sem=xrsem.at[i],
                device_id=y_partner,
                device_id_type=MESH,
            )
            for i, (src, dst) in enumerate(
                [(part_out, part_out_in), (part_stat, part_stat_in)]
            )
        ]

    for h in range(HEADS):
        cols, rows_ = pl.ds(h * T, T), pl.ds(h * T, T)
        pair, k = h // 2, h % 2
        before = precv[pair, pl.ds(QZ // 2 * k, QZ // 2)].reshape(T, T).astype(F32)
        tile = decay_of(srecv[pair, pl.ds(2 * T, 32)])[k]
        state = before * tall(tile, T) + srecv[pair, pl.ds(k * T, T)].astype(F32)
        carried = dot(lq[:, cols], state.astype(BF))
        light = within[h] + expcol[h] * carried
        mean = jnp.mean(light * light, axis=1, keepdims=True)
        out = (light * lax.rsqrt(mean + EPS) * gain_ref[h : h + 1, :]).astype(BF)
        lout_ref[:, cols] = out
        query = rotate(sq[:, cols].astype(F32) + out.astype(F32)).astype(BF)
        qown[rows_, :] = query
        high, low = split2(query.astype(F32) * SCALE)
        qhl[0, rows_, pl.ds(0, T)] = high
        qhl[0, rows_, pl.ds(T, T)] = low

    @pl.when(yh == 1)
    def _():
        each(0, HEADS, lambda h: q_copy(h).start())

    own_k, own_v = ks[0, x], vs[0, x]
    own_k2 = jnp.concatenate([own_k, own_k], axis=1)
    own_v2 = jnp.concatenate([own_v, jnp.ones_like(own_v)], axis=1)
    for h in range(HEADS):
        rows_ = pl.ds(h * T, T)
        scores = jnp.where(causal, nt_dot(qhl[0, rows_, :], own_k2), NEG)
        peak = jnp.broadcast_to(jnp.max(scores, axis=1, keepdims=True), (T, T))
        m_ref[0, rows_, :] = peak
        acc_ref[0, rows_, :] = dot(jnp.exp2(scores - peak).astype(BF), own_v2)

    @pl.when(yh == 0)
    def _():
        m_ref[1] = jnp.full((ROWS, T), NEG, F32)
        acc_ref[1] = jnp.zeros((ROWS, 2 * T), F32)

    wait_kz(3)
    send_kz(4)
    wait_vz(4)
    send_vx(3)
    send_vx(5)
    send_vx(4)
    for copy in cache_in:
        copy.wait_recv()

    def finish_rows(which, h):
        rows_ = pl.ds(h * T, T)
        return m_ref[which, rows_, :], acc_ref[which, rows_, 0:T], acc_ref[which, rows_, T : 2 * T]

    late = z // 4

    def job(v, carry):
        which = (1 - yh) * lax.rem(v // 2, 2)
        chunk = lax.rem(v, 2) + 2 * ((5 - v) // 4)
        mask = chunk + which * (4 - chunk)

        @pl.when(v == 2)
        def _():
            wait_kz(4)
            for copy in vx:
                copy.wait_recv()

        @pl.when((yh == 0) & (v == 2))
        def _():
            each(0, HEADS, lambda h: q_copy(h).wait_recv())
            high, low = split2(qpar[...].astype(F32) * SCALE)
            qhl[1, :, pl.ds(0, T)] = high
            qhl[1, :, pl.ds(T, T)] = low

        keys = ks[pl.ds(4 * chunk, 4)].reshape(CHUNK, T)
        keys2 = jnp.concatenate([keys, keys], axis=1)
        values = vs[pl.ds(4 * chunk, 4)].reshape(CHUNK, T)
        values2 = jnp.concatenate([values, jnp.ones_like(values)], axis=1)
        shade = bias[mask, 0:1, :]
        steps = ROWS // RB
        s_buf[0] = nt_dot(qhl[which, pl.ds(0, RB), :], keys2)
        for r in range(steps):
            rows_ = pl.ds(r * RB, RB)
            if r < steps - 1:
                s_buf[(r + 1) % 2] = nt_dot(qhl[which, pl.ds((r + 1) * RB, RB), :], keys2)
            scores = s_buf[r % 2] + shade
            best = scores[:, 0:T]
            for c in range(1, CHUNK // T):
                best = jnp.maximum(best, scores[:, c * T : (c + 1) * T])
            old = m_ref[which, rows_, :]
            new = jnp.maximum(old, jnp.max(best, axis=1, keepdims=True))
            shrink = jnp.exp2(old - new)
            m_ref[which, rows_, :] = new
            weights = jnp.exp2(scores - jnp.concatenate([new] * (CHUNK // T), axis=1)).astype(BF)
            acc_ref[which, rows_, :] = acc_ref[which, rows_, :] * jnp.concatenate(
                [shrink, shrink], axis=1
            ) + dot(weights, values2)

        @pl.when((yh == 0) & (v == 3))
        def _():
            for h in range(HEADS):
                peak, top, total = finish_rows(1, h)
                part_out[pl.ds(h * T, T), :] = (top / total).astype(BF)
                part_stat[pl.ds(h, 1), :] = (peak + jnp.log2(total)).T[0:1, :]
            for copy in back_copies():
                copy.start()

        return carry

    lax.fori_loop(0, 5 + late - 2 * yh, job, 0)

    @pl.when(yh == 0)
    def _():
        for h in range(HEADS):
            _, top, total = finish_rows(0, h)
            att_ref[:, pl.ds(h * T, T)] = (top / total).astype(BF)
        for copy in back_copies():
            copy.wait_send()

    @pl.when(yh == 1)
    def _():
        each(0, HEADS, lambda h: q_copy(h).wait_send())
        for copy in back_copies():
            copy.wait_recv()
        for h in range(HEADS):
            peak, top, total = finish_rows(0, h)
            other = jnp.broadcast_to(part_stat_in[pl.ds(h, 1), :], (T, T)).T
            best = jnp.maximum(peak, other)
            mine, theirs = jnp.exp2(peak - best), jnp.exp2(other - best)
            merged = top * mine + part_out_in[pl.ds(h * T, T), :].astype(F32) * theirs
            att_ref[:, pl.ds(h * T, T)] = (merged / (total * mine + theirs)).astype(BF)

    each(1, QZ, lambda d: t_copy(quarter_group(d)).wait_send())
    each(first_group + QZ, GROUPS, lambda g: t_copy(g).wait_send())
    each(1, QZ * NX, lambda d: p_copy(d).wait_send())
    copies.finish()


def per_device(lq, lk, lv, ld, gain, sq, skv, cache, lens, start):
    any_space = pl.BlockSpec(memory_space=pl.ANY)
    vmem = pl.BlockSpec(memory_space=pltpu.VMEM)
    smem = pl.BlockSpec(memory_space=pltpu.SMEM)
    rates = np.zeros((8, T), np.float32)
    rates[:, 0:32] = RATES
    rates[:, 32:64] = RATES
    scratch = [
        pltpu.VMEM((T, ROWS), BF),
        pltpu.VMEM((T, ROWS), BF),
        pltpu.VMEM((T, ROWS), BF),
        pltpu.VMEM((T, ROWS), BF),
        pltpu.VMEM((8 * 1024, T), BF),
        pltpu.VMEM((4, 2, 2, NX, T, T), BF),
        pltpu.VMEM((16, NX, T, T), BF),
        pltpu.VMEM((16, NX, T, T), BF),
        pltpu.VMEM((HEADS, T, T), F32),
        pltpu.VMEM((HEADS, T, T), F32),
        pltpu.VMEM((NX, 2 * T + 32, T), BF),
        pltpu.VMEM((NX, 2 * T + 32, T), BF),
        pltpu.VMEM((QZ, SLICE + 16, T), BF),
        pltpu.VMEM((GROUPS, SLICE + 16, T), BF),
        pltpu.VMEM((QZ, SLICE, T), BF),
        pltpu.VMEM((NX, QZ, SLICE, T), BF),
        pltpu.VMEM((NX, 2 * T + 32, T), BF),
        pltpu.VMEM((NX, 2 * T + 32, T), BF),
        pltpu.VMEM((ROWS, T), BF),
        pltpu.VMEM((ROWS, T), BF),
        pltpu.VMEM((2, ROWS, 2 * T), BF),
        pltpu.VMEM((5, 8, CHUNK), F32),
        pltpu.VMEM((2, ROWS, T), F32),
        pltpu.VMEM((2, ROWS, 2 * T), F32),
        pltpu.VMEM((2, RB, CHUNK), F32),
        pltpu.VMEM((ROWS, T), BF),
        pltpu.VMEM((HEADS, T), F32),
        pltpu.VMEM((ROWS, T), BF),
        pltpu.VMEM((HEADS, T), F32),
        pltpu.SemaphoreType.DMA((5,)),
        pltpu.SemaphoreType.DMA((N_COPIES,)),
        pltpu.SemaphoreType.DMA((N_COPIES,)),
        pltpu.SemaphoreType.DMA((GROUPS,)),
        pltpu.SemaphoreType.DMA((GROUPS,)),
        pltpu.SemaphoreType.DMA((QZ * NX,)),
        pltpu.SemaphoreType.DMA((QZ * NX,)),
        pltpu.SemaphoreType.DMA((2 + HEADS,)),
        pltpu.SemaphoreType.DMA((2 + HEADS,)),
        pltpu.SemaphoreType.REGULAR,
    ]
    return pl.pallas_call(
        kernel,
        out_shape=(
            jax.ShapeDtypeStruct((T, ROWS), BF),
            jax.ShapeDtypeStruct((T, ROWS), BF),
        ),
        in_specs=[
            any_space,
            any_space,
            any_space,
            vmem,
            vmem,
            any_space,
            vmem,
            any_space,
            vmem,
            smem,
            smem,
        ],
        out_specs=(vmem, vmem),
        scratch_shapes=scratch,
        compiler_params=pltpu.CompilerParams(
            collective_id=0, has_side_effects=True, vmem_limit_bytes=53 * 2**20
        ),
    )(
        lq,
        lk,
        lv,
        ld,
        gain.reshape(HEADS, T),
        sq,
        skv.reshape(2 * T, T),
        cache.reshape(8 * 1024, T),
        jnp.asarray(rates),
        lens,
        start,
    )


def solution(mesh):
    in_specs = (
        P("seq", "blk"),
        P("seq", "blk"),
        P("seq", "blk"),
        P("blk", "seq"),
        P("blk"),
        P("seq", "blk"),
        P("seq", None, "blk", None),
        P("blk", None, None, None),
        P(),
        P(),
    )
    out_specs = (P("seq", "blk"), P("seq", "blk"))
    return jax.shard_map(
        per_device, mesh=mesh, in_specs=in_specs, out_specs=out_specs, check_vma=False
    )
```

time: 67.4 us -> 66.5 us (0.987)
  Pallas kernels: 61.2 us -> 59 us
  local copies, waits for them, and re-layouts: 4.24 us -> 5.9 us
    unnamed x19 -> x14, local copies, waits for them, and re-layouts: 2.31 us -> 5.9 us
    pallas_call x1, Pallas kernels: 61.2 us -> 59 us  [per_device(): pl.pallas_call(kernel, out_shape=(jax.ShapeDtypeStruct((T, ROWS), BF), ja...]
    transpose x1 -> x0, local copies, waits for them, and re-layouts: 1.94 us -> none  [per_device(): cache_t = cache.transpose(2, 1, 0, 3).reshape(4, 2, 2, NX, T, T)]
where the time goes in v2:
time: 66.5 us; the launch traced here: 66.2 us
  Pallas kernels  59 us (89%)
  local copies, waits for them, and re-layouts  5.9 us (9%)
  between operations  1.3 us (2%)
    pallas_call x1, Pallas kernels, per_device(): pl.pallas_call(kernel, out_shape=(jax.ShapeDtypeStruct((T, ROWS), BF), ja...  59 us
    unnamed x14, local copies, waits for them, and re-layouts  5.9 us

profile of v2, /device:TPU:16, one launch (start us, length us, event | category | flops | bytes accessed | tf_op | source)
XLA Modules:
  0.0 66.2 jit_solution(15577140411464004733)
XLA Ops:
  1.3 0.0 copy-start
  1.3 0.9 %copy-done = bf16[128,1024]{1,0:T(8,128)(2,1)S(1)} copy-done((bf16[128,1024]{1,0:T(8,128)(2,1)S(1)}, bf16[128,1024]{1,0:T(8,128)(2,1)}, u32[]{:S(2)}) %copy-start) | copy-done | bytes 262168
  2.2 0.0 copy-start.1
  2.2 0.8 %copy-done.1 = bf16[128,2,1,128]{3,1,2,0:T(2,128)(2,1)S(1)} copy-done((bf16[128,2,1,128]{3,1,2,0:T(2,128)(2,1)S(1)}, bf16[128,2,1,128]{3,1,2,0:T(2,128)(2,1)}, u32[]{:S(2)}) %copy-start.1) | copy-done | bytes 65560
  3.1 0.0 copy-start.2
  3.1 0.7 %copy-done.2 = f32[8,128]{1,0:T(8,128)S(1)} copy-done((f32[8,128]{1,0:T(8,128)S(1)}, f32[8,128]{1,0:T(8,128)}, u32[]{:S(2)}) %copy-start.2) | copy-done | bytes 4120
  3.8 0.0 copy-start.3
  3.8 0.7 %copy-done.3 = f32[1024]{0:T(1024)S(1)} copy-done((f32[1024]{0:T(1024)S(1)}, f32[1024]{0:T(1024)}, u32[]{:S(2)}) %copy-start.3) | copy-done | bytes 4120
  4.4 0.0 copy-start.4
  4.4 0.7 %copy-done.4 = f32[8,128]{1,0:T(8,128)S(1)} copy-done((f32[8,128]{1,0:T(8,128)S(1)}, f32[8,128]{1,0:T(8,128)}, u32[]{:S(2)}) %copy-start.4) | copy-done | bytes 4120
  5.1 0.0 copy-start.5
  5.1 0.7 copy-done.5
  5.8 59.0 %shard_map.122 = (bf16[128,1024]{1,0:T(8,128)(2,1)S(1)}, bf16[128,1024]{1,0:T(8,128)(2,1)S(1)}) custom-call(bf16[128,1024]{1,0:T(8,128)(2,1)S(1)} %copy-done, bf16[128,1024]{1,0:T(8,128)(2,1)} %lk_hbm.1, bf16[128,1024]{1,0:T(8,128)(2,1)} %lv_hbm.1, f32[8,128]{1,0:T(8,128)S(1)} %copy-done.2, f32[8,128]{1,0:T(8,128)S(1)} %bitcast.4, bf16[128,1024]{1,0:T(8,128)(2,1)} %sq_hbm.1, ...), custom_call_target="tpu_custom_call" | custom-call | tf_op jit(solution)/shard_map/pallas_call | solution.py:666
  64.8 0.7 %copy.16 = bf16[128,1024]{1,0:T(8,128)(2,1)} copy(bf16[128,1024]{1,0:T(8,128)(2,1)S(1)} %get-tuple-element.4) | data formatting | bytes 524288
  65.5 0.7 %copy.17 = bf16[128,1024]{1,0:T(8,128)(2,1)} copy(bf16[128,1024]{1,0:T(8,128)(2,1)S(1)} %get-tuple-element.5) | data formatting | bytes 524288
Async XLA Ops:
  1.3 1.0 %copy-start = (bf16[128,1024]{1,0:T(8,128)(2,1)S(1)}, bf16[128,1024]{1,0:T(8,128)(2,1)}, u32[]{:S(2)}) copy-start(bf16[128,1024]{1,0:T(8,128)(2,1)} %lq_hbm.1) | copy-start | bytes 786436
  2.2 0.8 %copy-start.1 = (bf16[128,2,1,128]{3,1,2,0:T(2,128)(2,1)S(1)}, bf16[128,2,1,128]{3,1,2,0:T(2,128)(2,1)}, u32[]{:S(2)}) copy-start(bf16[128,2,1,128]{3,1,2,0:T(2,128)(2,1)} %param.17) | copy-start | bytes 196612
  3.1 0.7 %copy-start.2 = (f32[8,128]{1,0:T(8,128)S(1)}, f32[8,128]{1,0:T(8,128)}, u32[]{:S(2)}) copy-start(f32[8,128]{1,0:T(8,128)} %ld_ref.1) | copy-start | bytes 12292
  3.8 0.7 %copy-start.3 = (f32[1024]{0:T(1024)S(1)}, f32[1024]{0:T(1024)}, u32[]{:S(2)}) copy-start(f32[1024]{0:T(1024)} %param.15) | copy-start | bytes 12292
  4.4 0.7 %copy-start.4 = (f32[8,128]{1,0:T(8,128)S(1)}, f32[8,128]{1,0:T(8,128)}, u32[]{:S(2)}) copy-start(f32[8,128]{1,0:T(8,128)} %constant.2.clone.rates_ref) | copy-start | bytes 12292
  5.1 0.7 copy-start.5

commit v3 on v2

--- a/solution.py
+++ b/solution.py
@@ -83,12 +83,12 @@
     lq_hbm,
     lk_hbm,
     lv_hbm,
-    ld_ref,
-    gain_ref,
+    ld_hbm,
+    gain_hbm,
     sq_hbm,
-    skv_ref,
+    skv_hbm,
     cache_hbm,
-    rates_ref,
+    rates_hbm,
     lens_ref,
     start_ref,
     lout_ref,
@@ -122,6 +122,12 @@
     part_stat,
     part_out_in,
     part_stat_in,
+    lout,
+    att,
+    ld,
+    skv,
+    gain,
+    rates,
     lsem,
     ssem,
     rsem,
@@ -167,6 +173,25 @@
 
         lax.fori_loop(first, last, one, 0)
 
+    loads = [
+        pltpu.make_async_copy(src, dst, lsem.at[i])
+        for i, (src, dst) in enumerate(
+            [
+                (lk_hbm, lk),
+                (lv_hbm, lv),
+                (lq_hbm, lq),
+                (sq_hbm, sq),
+                (cache_hbm, cache_raw),
+                (ld_hbm, ld),
+                (skv_hbm, skv),
+                (gain_hbm, gain),
+                (rates_hbm, rates),
+            ]
+        )
+    ]
+    for i in (5, 0, 1, 6, 8, 2, 4, 3, 7):
+        loads[i].start()
+
     barrier = pltpu.get_barrier_semaphore()
 
     def greet(device):
@@ -179,16 +204,8 @@
             greet(at(yh_, z, x, (1 - yl) * 2 + core_))
     each(first_group + QZ, GROUPS, lambda g: greet(column(g)))
 
-    loads = [
-        pltpu.make_async_copy(src, dst, lsem.at[i])
-        for i, (src, dst) in enumerate(
-            [(lk_hbm, lk), (lv_hbm, lv), (lq_hbm, lq), (sq_hbm, sq), (cache_hbm, cache_raw)]
-        )
-    ]
-    for load in loads:
-        load.start()
-
-    cumulative = ld_ref[...]
+    loads[5].wait()
+    cumulative = ld[...]
     lane8 = lax.broadcasted_iota(jnp.int32, (HEADS, T), 1)
     shift = 1
     while shift < T:
@@ -213,22 +230,6 @@
         lsend[pair, pl.ds(2 * T, 32)] = jnp.concatenate(rows_, axis=0).astype(BF)
     lrecv[x] = lsend[x]
 
-    lane = lax.broadcasted_iota(jnp.int32, (T, T), 1)
-    row = lax.broadcasted_iota(jnp.int32, (T, T), 0)
-    positions = (start_ref[0] + seq * T + row).astype(F32)
-    angles = positions * rates_ref[0:1, :]
-    sine = jnp.sin(angles)
-    cos_t = jnp.where(lane < 64, jnp.cos(angles), 1.0)
-    sin_t = jnp.where(lane < 32, -sine, jnp.where(lane < 64, sine, 0.0))
-
-    def rotate(features):
-        partner = jnp.where(lane < 32, pltpu.roll(features, 96, 1), pltpu.roll(features, 32, 1))
-        return features * cos_t + partner * sin_t
-
-    span = dot(one_hot(2, T), skv_ref[...])
-    ks[0, x] = rotate(span[0:T]).astype(BF)
-    vs[0, x] = span[T : 2 * T].astype(BF)
-
     pl.semaphore_wait(barrier, QZ * NX - 1 + 5 + first_group)
     each(
         0,
@@ -240,6 +241,24 @@
     lx = [
         copies.start(lsend.at[lax.rem(x + d, NX)], lrecv.at[x], x_peer(d)) for d in range(1, NX)
     ]
+
+    lane = lax.broadcasted_iota(jnp.int32, (T, T), 1)
+    row = lax.broadcasted_iota(jnp.int32, (T, T), 0)
+    loads[8].wait()
+    loads[6].wait()
+    positions = (start_ref[0] + seq * T + row).astype(F32)
+    angles = positions * rates[0:1, :]
+    sine = jnp.sin(angles)
+    cos_t = jnp.where(lane < 64, jnp.cos(angles), 1.0)
+    sin_t = jnp.where(lane < 32, -sine, jnp.where(lane < 64, sine, 0.0))
+
+    def rotate(features):
+        partner = jnp.where(lane < 32, pltpu.roll(features, 96, 1), pltpu.roll(features, 32, 1))
+        return features * cos_t + partner * sin_t
+
+    span = dot(one_hot(2, T), skv[...])
+    ks[0, x] = rotate(span[0:T]).astype(BF)
+    vs[0, x] = span[T : 2 * T].astype(BF)
 
     vz, vx, kz = {}, [], {}
 
@@ -285,6 +304,16 @@
         scores = nt_dot(lq[:, cols], lk[:, cols])
         within[h] = dot((scores * weights).astype(BF), lv[:, cols])
         expcol[h] = jnp.exp(downward)
+
+    @pl.when(quarter < 3)
+    def _():
+        pl.semaphore_wait(ready, GROUPS - QZ - first_group)
+
+    send_vz(1)
+    send_vx(0)
+    for copy in kx:
+        copy.wait_recv()
+    send_kz(1)
 
     for copy in lx:
         copy.wait_recv()
@@ -343,22 +372,12 @@
         return first_group + lax.rem(zq + d, QZ)
 
     each(1, QZ, lambda d: t_copy(quarter_group(d)).start())
+    each(first_group + QZ, GROUPS, lambda g: t_copy(g).start())
     trecv[group] = tsend[zq]
     sx = [
         copies.start(ssend.at[lax.rem(x + d, NX)], srecv.at[x], x_peer(d)) for d in range(1, NX)
     ]
     srecv[x] = ssend[x]
-
-    @pl.when(quarter < 3)
-    def _():
-        pl.semaphore_wait(ready, GROUPS - QZ - first_group)
-
-    each(first_group + QZ, GROUPS, lambda g: t_copy(g).start())
-    send_vz(1)
-    send_vx(0)
-    for copy in kx:
-        copy.wait_recv()
-    send_kz(1)
 
     loads[4].wait()
     sort = one_hot(8, 32)
@@ -454,6 +473,7 @@
     for copy in sx:
         copy.wait_recv()
     loads[3].wait()
+    loads[7].wait()
     each(1, QZ * NX, lambda d: p_copy(d).wait_recv())
 
     def q_copy(h):
@@ -461,25 +481,28 @@
         return pltpu.make_async_remote_copy(
             src_ref=qown.at[rows_],
             dst_ref=qpar.at[rows_],
-            send_sem=xsem.at[2 + h],
-            recv_sem=xrsem.at[2 + h],
+            send_sem=xsem.at[h],
+            recv_sem=xrsem.at[h],
             device_id=y_partner,
             device_id_type=MESH,
         )
 
-    def back_copies():
+    def back_copies(half):
+        rows_ = pl.ds(half * (ROWS // 2), ROWS // 2)
+        pairs = [
+            (part_out.at[rows_], part_out_in.at[rows_]),
+            (part_stat.at[half], part_stat_in.at[half]),
+        ]
         return [
             pltpu.make_async_remote_copy(
                 src_ref=src,
                 dst_ref=dst,
-                send_sem=xsem.at[i],
-                recv_sem=xrsem.at[i],
+                send_sem=xsem.at[HEADS + 2 * half + i],
+                recv_sem=xrsem.at[HEADS + 2 * half + i],
                 device_id=y_partner,
                 device_id_type=MESH,
             )
-            for i, (src, dst) in enumerate(
-                [(part_out, part_out_in), (part_stat, part_stat_in)]
-            )
+            for i, (src, dst) in enumerate(pairs)
         ]
 
     for h in range(HEADS):
@@ -491,8 +514,8 @@
         carried = dot(lq[:, cols], state.astype(BF))
         light = within[h] + expcol[h] * carried
         mean = jnp.mean(light * light, axis=1, keepdims=True)
-        out = (light * lax.rsqrt(mean + EPS) * gain_ref[h : h + 1, :]).astype(BF)
-        lout_ref[:, cols] = out
+        out = (light * lax.rsqrt(mean + EPS) * gain[h : h + 1, :]).astype(BF)
+        lout[:, cols] = out
         query = rotate(sq[:, cols].astype(F32) + out.astype(F32)).astype(BF)
         qown[rows_, :] = query
         high, low = split2(query.astype(F32) * SCALE)
@@ -502,6 +525,9 @@
     @pl.when(yh == 1)
     def _():
         each(0, HEADS, lambda h: q_copy(h).start())
+
+    lout_out = pltpu.make_async_copy(lout, lout_ref, lsem.at[9])
+    lout_out.start()
 
     own_k, own_v = ks[0, x], vs[0, x]
     own_k2 = jnp.concatenate([own_k, own_k], axis=1)
@@ -537,6 +563,7 @@
         which = (1 - yh) * lax.rem(v // 2, 2)
         chunk = lax.rem(v, 2) + 2 * ((5 - v) // 4)
         mask = chunk + which * (4 - chunk)
+        half = v - 2
 
         @pl.when(v == 2)
         def _():
@@ -544,24 +571,35 @@
             for copy in vx:
                 copy.wait_recv()
 
-        @pl.when((yh == 0) & (v == 2))
-        def _():
-            each(0, HEADS, lambda h: q_copy(h).wait_recv())
-            high, low = split2(qpar[...].astype(F32) * SCALE)
-            qhl[1, :, pl.ds(0, T)] = high
-            qhl[1, :, pl.ds(T, T)] = low
-
-        keys = ks[pl.ds(4 * chunk, 4)].reshape(CHUNK, T)
-        keys2 = jnp.concatenate([keys, keys], axis=1)
-        values = vs[pl.ds(4 * chunk, 4)].reshape(CHUNK, T)
-        values2 = jnp.concatenate([values, jnp.ones_like(values)], axis=1)
+        for i in range(2):
+
+            @pl.when((yh == 0) & (v == 2 + i))
+            def _():
+                each(4 * i, 4 * i + 4, lambda h: q_copy(h).wait_recv())
+                rows_ = pl.ds(i * (ROWS // 2), ROWS // 2)
+                high, low = split2(qpar[rows_].astype(F32) * SCALE)
+                qhl[1, rows_, pl.ds(0, T)] = high
+                qhl[1, rows_, pl.ds(T, T)] = low
+
+        def place(step):
+            own, other = step * RB, half * (ROWS // 2) + step % 2 * RB
+            start_row = pl.multiple_of((1 - which) * own + which * other, RB)
+            return pl.ds(start_row, RB), (1 - which) * chunk + which * (step // 2)
+
+        def score(step):
+            rows_, part = place(step)
+            keys = ks[pl.ds(4 * part, 4)].reshape(CHUNK, T)
+            return nt_dot(qhl[which, rows_, :], jnp.concatenate([keys, keys], axis=1))
+
         shade = bias[mask, 0:1, :]
         steps = ROWS // RB
-        s_buf[0] = nt_dot(qhl[which, pl.ds(0, RB), :], keys2)
+        s_buf[0] = score(0)
         for r in range(steps):
-            rows_ = pl.ds(r * RB, RB)
+            rows_, part = place(r)
             if r < steps - 1:
-                s_buf[(r + 1) % 2] = nt_dot(qhl[which, pl.ds((r + 1) * RB, RB), :], keys2)
+                s_buf[(r + 1) % 2] = score(r + 1)
+            values = vs[pl.ds(4 * part, 4)].reshape(CHUNK, T)
+            values2 = jnp.concatenate([values, jnp.ones_like(values)], axis=1)
             scores = s_buf[r % 2] + shade
             best = scores[:, 0:T]
             for c in range(1, CHUNK // T):
@@ -575,14 +613,18 @@
                 [shrink, shrink], axis=1
             ) + dot(weights, values2)
 
-        @pl.when((yh == 0) & (v == 3))
-        def _():
-            for h in range(HEADS):
-                peak, top, total = finish_rows(1, h)
-                part_out[pl.ds(h * T, T), :] = (top / total).astype(BF)
-                part_stat[pl.ds(h, 1), :] = (peak + jnp.log2(total)).T[0:1, :]
-            for copy in back_copies():
-                copy.start()
+        for i in range(2):
+
+            @pl.when((yh == 0) & (v == 2 + i))
+            def _():
+                stats = []
+                for h in range(4 * i, 4 * i + 4):
+                    peak, top, total = finish_rows(1, h)
+                    part_out[pl.ds(h * T, T), :] = (top / total).astype(BF)
+                    stats.append((peak + jnp.log2(total)).T[0:1, :])
+                part_stat[i] = jnp.concatenate(stats + stats, axis=0)
+                for copy in back_copies(i):
+                    copy.start()
 
         return carry
 
@@ -592,32 +634,50 @@
     def _():
         for h in range(HEADS):
             _, top, total = finish_rows(0, h)
-            att_ref[:, pl.ds(h * T, T)] = (top / total).astype(BF)
-        for copy in back_copies():
+            att[:, pl.ds(h * T, T)] = (top / total).astype(BF)
+        for copy in back_copies(0) + back_copies(1):
             copy.wait_send()
 
     @pl.when(yh == 1)
     def _():
         each(0, HEADS, lambda h: q_copy(h).wait_send())
-        for copy in back_copies():
+        for copy in back_copies(0) + back_copies(1):
             copy.wait_recv()
         for h in range(HEADS):
             peak, top, total = finish_rows(0, h)
-            other = jnp.broadcast_to(part_stat_in[pl.ds(h, 1), :], (T, T)).T
+            other = jnp.broadcast_to(part_stat_in[h // 4, pl.ds(h % 4, 1), :], (T, T)).T
             best = jnp.maximum(peak, other)
             mine, theirs = jnp.exp2(peak - best), jnp.exp2(other - best)
             merged = top * mine + part_out_in[pl.ds(h * T, T), :].astype(F32) * theirs
-            att_ref[:, pl.ds(h * T, T)] = (merged / (total * mine + theirs)).astype(BF)
-
+            att[:, pl.ds(h * T, T)] = (merged / (total * mine + theirs)).astype(BF)
+
+    att_out = pltpu.make_async_copy(att, att_ref, lsem.at[10])
+    att_out.start()
     each(1, QZ, lambda d: t_copy(quarter_group(d)).wait_send())
     each(first_group + QZ, GROUPS, lambda g: t_copy(g).wait_send())
     each(1, QZ * NX, lambda d: p_copy(d).wait_send())
     copies.finish()
+    lout_out.wait()
+    att_out.wait()
+
+
+def emit(a_ref, b_ref, a_out, b_out, a_held, b_held, sem):
+    pairs = ((a_ref, a_held, a_out), (b_ref, b_held, b_out))
+    ins = [pltpu.make_async_copy(src, held, sem.at[i]) for i, (src, held, _) in enumerate(pairs)]
+    outs = [
+        pltpu.make_async_copy(held, dst, sem.at[2 + i]) for i, (_, held, dst) in enumerate(pairs)
+    ]
+    for move in ins:
+        move.start()
+    for i in range(2):
+        ins[i].wait()
+        outs[i].start()
+    for move in outs:
+        move.wait()
 
 
 def per_device(lq, lk, lv, ld, gain, sq, skv, cache, lens, start):
     any_space = pl.BlockSpec(memory_space=pl.ANY)
-    vmem = pl.BlockSpec(memory_space=pltpu.VMEM)
     smem = pl.BlockSpec(memory_space=pltpu.SMEM)
     rates = np.zeros((8, T), np.float32)
     rates[:, 0:32] = RATES
@@ -649,43 +709,37 @@
         pltpu.VMEM((2, ROWS, 2 * T), F32),
         pltpu.VMEM((2, RB, CHUNK), F32),
         pltpu.VMEM((ROWS, T), BF),
+        pltpu.VMEM((2, 8, T), F32),
+        pltpu.VMEM((ROWS, T), BF),
+        pltpu.VMEM((2, 8, T), F32),
+        pltpu.VMEM((T, ROWS), BF),
+        pltpu.VMEM((T, ROWS), BF),
         pltpu.VMEM((HEADS, T), F32),
-        pltpu.VMEM((ROWS, T), BF),
+        pltpu.VMEM((2 * T, T), BF),
         pltpu.VMEM((HEADS, T), F32),
-        pltpu.SemaphoreType.DMA((5,)),
+        pltpu.VMEM((8, T), F32),
+        pltpu.SemaphoreType.DMA((11,)),
         pltpu.SemaphoreType.DMA((N_COPIES,)),
         pltpu.SemaphoreType.DMA((N_COPIES,)),
         pltpu.SemaphoreType.DMA((GROUPS,)),
         pltpu.SemaphoreType.DMA((GROUPS,)),
         pltpu.SemaphoreType.DMA((QZ * NX,)),
         pltpu.SemaphoreType.DMA((QZ * NX,)),
-        pltpu.SemaphoreType.DMA((2 + HEADS,)),
-        pltpu.SemaphoreType.DMA((2 + HEADS,)),
+        pltpu.SemaphoreType.DMA((4 + HEADS,)),
+        pltpu.SemaphoreType.DMA((4 + HEADS,)),
         pltpu.SemaphoreType.REGULAR,
     ]
-    return pl.pallas_call(
+    results = pl.pallas_call(
         kernel,
         out_shape=(
             jax.ShapeDtypeStruct((T, ROWS), BF),
             jax.ShapeDtypeStruct((T, ROWS), BF),
         ),
-        in_specs=[
-            any_space,
-            any_space,
-            any_space,
-            vmem,
-            vmem,
-            any_space,
-            vmem,
-            any_space,
-            vmem,
-            smem,
-            smem,
-        ],
-        out_specs=(vmem, vmem),
+        in_specs=[any_space] * 9 + [smem, smem],
+        out_specs=(any_space, any_space),
         scratch_shapes=scratch,
         compiler_params=pltpu.CompilerParams(
-            collective_id=0, has_side_effects=True, vmem_limit_bytes=53 * 2**20
+            collective_id=0, has_side_effects=True, vmem_limit_bytes=60 * 2**20
         ),
     )(
         lq,
@@ -700,6 +754,13 @@
         lens,
         start,
     )
+    return pl.pallas_call(
+        emit,
+        out_shape=tuple(jax.ShapeDtypeStruct(r.shape, r.dtype) for r in results),
+        in_specs=[any_space, any_space],
+        out_specs=(any_space, any_space),
+        scratch_shapes=[pltpu.VMEM((T, ROWS), BF), pltpu.VMEM((T, ROWS), BF), pltpu.SemaphoreType.DMA((4,))],
+    )(*results)
 
 
 def solution(mesh):

time: 66.5 us -> 61.4 us (0.923)
  local copies, waits for them, and re-layouts: 5.9 us -> 0 us
  Pallas kernels: 59 us -> 60 us
    unnamed x14 -> x0, local copies, waits for them, and re-layouts: 5.9 us -> none
    pallas_call x0 -> x1, Pallas kernels: none -> 1.77 us  [per_device(): pl.pallas_call(emit, out_shape=tuple((jax.ShapeDtypeStruct(r.shape, r.dty...]
    pallas_call x1, Pallas kernels: 59 us -> 58.2 us  [per_device(): pl.pallas_call(kernel, out_shape=(jax.ShapeDtypeStruct((T, ROWS), BF), ja...]
where the time goes in v3:
time: 61.4 us; the launch traced here: 61.3 us
  Pallas kernels  60 us (98%)
  between operations  1.29 us (2%)
    pallas_call x1, Pallas kernels, per_device(): pl.pallas_call(kernel, out_shape=(jax.ShapeDtypeStruct((T, ROWS), BF), ja...  58.2 us
    pallas_call x1, Pallas kernels, per_device(): pl.pallas_call(emit, out_shape=tuple((jax.ShapeDtypeStruct(r.shape, r.dty...  1.77 us

profile of v3, /device:TPU:16, one launch (start us, length us, event | category | flops | bytes accessed | tf_op | source)
XLA Modules:
  0.0 61.3 jit_solution(5488196181769190061)
XLA Ops:
  1.3 58.2 %shard_map.122 = (bf16[128,1024]{1,0:T(8,128)(2,1)}, bf16[128,1024]{1,0:T(8,128)(2,1)}) custom-call(bf16[128,1024]{1,0:T(8,128)(2,1)} %lq_hbm.1, bf16[128,1024]{1,0:T(8,128)(2,1)} %lk_hbm.1, bf16[128,1024]{1,0:T(8,128)(2,1)} %lv_hbm.1, f32[8,128]{1,0:T(8,128)} %ld_hbm.1, f32[8,128]{1,0:T(8,128)} %bitcast.5, bf16[128,1024]{1,0:T(8,128)(2,1)} %sq_hbm.1, ...), custom_call_target="tpu_custom_call" | custom-call | tf_op jit(solution)/shard_map/pallas_call | solution.py:732
  59.5 1.8 %shard_map.123 = (bf16[128,1024]{1,0:T(8,128)(2,1)}, bf16[128,1024]{1,0:T(8,128)(2,1)}) custom-call(bf16[128,1024]{1,0:T(8,128)(2,1)} %get-tuple-element.4.a_ref, bf16[128,1024]{1,0:T(8,128)(2,1)} %get-tuple-element.5.b_ref), custom_call_target="tpu_custom_call" | custom-call | tf_op jit(solution)/shard_map/pallas_call | solution.py:757

commit v4 on v3

--- a/solution.py
+++ b/solution.py
@@ -99,8 +99,7 @@
     sq,
     cache_raw,
     cache,
-    ks,
-    vs,
+    kv,
     within,
     expcol,
     lsend,
@@ -257,42 +256,31 @@
         return features * cos_t + partner * sin_t
 
     span = dot(one_hot(2, T), skv[...])
-    ks[0, x] = rotate(span[0:T]).astype(BF)
-    vs[0, x] = span[T : 2 * T].astype(BF)
-
-    vz, vx, kz = {}, [], {}
-
-    def send_vz(step):
+    kv[0, x, 0] = rotate(span[0:T]).astype(BF)
+    kv[0, x, 1] = span[T : 2 * T].astype(BF)
+
+    along_z, along_x = {}, []
+
+    def send_z(step):
         if step < 4:
-            vz["u", step] = copies.start(vs.at[step - 1, x], vs.at[step, x], up)
-            vz["d", step] = copies.start(vs.at[(9 - step) % 8, x], vs.at[8 - step, x], down)
+            moves = [
+                copies.start(kv.at[step - 1, x], kv.at[step, x], up),
+                copies.start(kv.at[(9 - step) % 8, x], kv.at[8 - step, x], down),
+            ]
         else:
-            first, last_ = pl.ds(0, T // 2), pl.ds(T // 2, T // 2)
-            vz["u", step] = copies.start(vs.at[3, x, first], vs.at[4, x, first], up)
-            vz["d", step] = copies.start(vs.at[5, x, last_], vs.at[4, x, last_], down)
-
-    def wait_vz(step):
-        vz["u", step].wait_recv()
-        vz["d", step].wait_recv()
-
-    def send_vx(slot):
+            moves = [
+                copies.start(kv.at[3, x, 0], kv.at[4, x, 0], up),
+                copies.start(kv.at[5, x, 1], kv.at[4, x, 1], down),
+            ]
+        along_z[step] = moves
+
+    def wait_z(step):
+        for copy in along_z[step]:
+            copy.wait_recv()
+
+    def send_x(slot):
         for d in range(1, NX):
-            vx.append(copies.start(vs.at[slot, x], vs.at[slot, x], x_peer(d)))
-
-    def send_kz(step):
-        if step < 4:
-            kz["u", step] = copies.start(ks.at[step - 1], ks.at[step], up)
-            kz["d", step] = copies.start(ks.at[(9 - step) % 8], ks.at[8 - step], down)
-        else:
-            first, last_ = pl.ds(0, 2), pl.ds(2, 2)
-            kz["u", step] = copies.start(ks.at[3, first], ks.at[4, first], up)
-            kz["d", step] = copies.start(ks.at[5, last_], ks.at[4, last_], down)
-
-    def wait_kz(step):
-        kz["u", step].wait_recv()
-        kz["d", step].wait_recv()
-
-    kx = [copies.start(ks.at[0, x], ks.at[0, x], x_peer(d)) for d in range(1, NX)]
+            along_x.append(copies.start(kv.at[slot, x], kv.at[slot, x], x_peer(d)))
 
     causal = row >= lane
     loads[2].wait()
@@ -305,15 +293,26 @@
         within[h] = dot((scores * weights).astype(BF), lv[:, cols])
         expcol[h] = jnp.exp(downward)
 
+    loads[4].wait()
+    sort = one_hot(8, 32)
+
+    def relayout(b, carry):
+        part = dot(sort, cache_raw[pl.ds(pl.multiple_of(b * 256, 256), 256), :]).astype(BF)
+        rows_ = pl.ds(pl.multiple_of(lax.rem(b, 4) * 32, 32), 32)
+        for i in range(2):
+            for h in range(4):
+                at_ = (i * 4 + h) * 32
+                cache[h, b // 16, lax.rem(b // 4, 4), i, rows_] = part[at_ : at_ + 32]
+        return carry
+
+    lax.fori_loop(0, 32, relayout, 0, unroll=4)
+
     @pl.when(quarter < 3)
     def _():
         pl.semaphore_wait(ready, GROUPS - QZ - first_group)
 
-    send_vz(1)
-    send_vx(0)
-    for copy in kx:
-        copy.wait_recv()
-    send_kz(1)
+    send_z(1)
+    send_x(0)
 
     for copy in lx:
         copy.wait_recv()
@@ -379,42 +378,24 @@
     ]
     srecv[x] = ssend[x]
 
-    loads[4].wait()
-    sort = one_hot(8, 32)
-
-    def relayout(b, carry):
-        part = dot(sort, cache_raw[pl.ds(pl.multiple_of(b * 256, 256), 256), :]).astype(BF)
-        rows_ = pl.ds(pl.multiple_of(lax.rem(b, 4) * 32, 32), 32)
-        for kv in range(2):
-            for h in range(4):
-                at_ = (kv * 4 + h) * 32
-                cache[h, kv, b // 16, lax.rem(b // 4, 4), rows_] = part[at_ : at_ + 32]
-        return carry
-
-    lax.fori_loop(0, 32, relayout, 0, unroll=4)
-
-    cache_in = []
-    for kv, buf in ((0, ks), (1, vs)):
-        cache_in.append(
-            copies.start(cache.at[sibling, kv], buf.at[pl.ds(8 + 2 * blk, 2)], (seq, sibling))
-        )
-        for flip in range(2):
-            for swap in range(2):
-                yh_ = yh + flip - 2 * flip * yh
-                other = (1 - yl) * 2 + core + swap - 2 * swap * core
-                cache_in.append(
-                    copies.start(
-                        cache.at[other, kv, yh],
-                        buf.at[8 + 2 * blk + yh],
-                        at(yh_, z, x, other),
-                    )
+    cache_in = [
+        copies.start(cache.at[sibling], kv.at[pl.ds(8 + 2 * blk, 2)], (seq, sibling))
+    ]
+    for flip in range(2):
+        for swap in range(2):
+            yh_ = yh + flip - 2 * flip * yh
+            other = (1 - yl) * 2 + core + swap - 2 * swap * core
+            cache_in.append(
+                copies.start(
+                    cache.at[other, yh], kv.at[8 + 2 * blk + yh], at(yh_, z, x, other)
                 )
-        buf[pl.ds(8 + 2 * blk, 2)] = cache[blk, kv]
-
-    wait_vz(1)
-    send_vz(2)
-    wait_kz(1)
-    send_kz(2)
+            )
+    kv[pl.ds(8 + 2 * blk, 2)] = cache[blk]
+
+    wait_z(1)
+    send_z(2)
+    send_x(1)
+    send_x(7)
 
     def chain(g, state):
         tile = trecv[g, pl.ds(SLICE, 16)].astype(F32)
@@ -445,12 +426,10 @@
     each(1, QZ * NX, lambda d: p_copy(d).start())
     precv[x, zq] = psend[zq]
 
-    wait_vz(2)
-    send_vz(3)
-    send_vx(1)
-    send_vx(7)
-    wait_kz(2)
-    send_kz(3)
+    wait_z(2)
+    send_z(3)
+    send_x(2)
+    send_x(6)
 
     col = lax.broadcasted_iota(jnp.int32, (8, CHUNK), 1)
     visible_to = 512 * (z + 1)
@@ -465,16 +444,18 @@
         )
     bias[4] = jnp.zeros((8, CHUNK), F32)
 
-    wait_vz(3)
-    send_vz(4)
-    send_vx(2)
-    send_vx(6)
+    wait_z(3)
+    send_z(4)
+    send_x(3)
+    send_x(5)
 
     for copy in sx:
         copy.wait_recv()
     loads[3].wait()
     loads[7].wait()
     each(1, QZ * NX, lambda d: p_copy(d).wait_recv())
+    wait_z(4)
+    send_x(4)
 
     def q_copy(h):
         rows_ = pl.ds(h * T, T)
@@ -529,7 +510,7 @@
     lout_out = pltpu.make_async_copy(lout, lout_ref, lsem.at[9])
     lout_out.start()
 
-    own_k, own_v = ks[0, x], vs[0, x]
+    own_k, own_v = kv[0, x, 0], kv[0, x, 1]
     own_k2 = jnp.concatenate([own_k, own_k], axis=1)
     own_v2 = jnp.concatenate([own_v, jnp.ones_like(own_v)], axis=1)
     for h in range(HEADS):
@@ -544,12 +525,6 @@
         m_ref[1] = jnp.full((ROWS, T), NEG, F32)
         acc_ref[1] = jnp.zeros((ROWS, 2 * T), F32)
 
-    wait_kz(3)
-    send_kz(4)
-    wait_vz(4)
-    send_vx(3)
-    send_vx(5)
-    send_vx(4)
     for copy in cache_in:
         copy.wait_recv()
 
@@ -567,8 +542,7 @@
 
         @pl.when(v == 2)
         def _():
-            wait_kz(4)
-            for copy in vx:
+            for copy in along_x:
                 copy.wait_recv()
 
         for i in range(2):
@@ -588,7 +562,7 @@
 
         def score(step):
             rows_, part = place(step)
-            keys = ks[pl.ds(4 * part, 4)].reshape(CHUNK, T)
+            keys = kv[pl.ds(4 * part, 4), :, 0].reshape(CHUNK, T)
             return nt_dot(qhl[which, rows_, :], jnp.concatenate([keys, keys], axis=1))
 
         shade = bias[mask, 0:1, :]
@@ -598,7 +572,7 @@
             rows_, part = place(r)
             if r < steps - 1:
                 s_buf[(r + 1) % 2] = score(r + 1)
-            values = vs[pl.ds(4 * part, 4)].reshape(CHUNK, T)
+            values = kv[pl.ds(4 * part, 4), :, 1].reshape(CHUNK, T)
             values2 = jnp.concatenate([values, jnp.ones_like(values)], axis=1)
             scores = s_buf[r % 2] + shade
             best = scores[:, 0:T]
@@ -662,15 +636,18 @@
 
 
 def emit(a_ref, b_ref, a_out, b_out, a_held, b_held, sem):
-    pairs = ((a_ref, a_held, a_out), (b_ref, b_held, b_out))
-    ins = [pltpu.make_async_copy(src, held, sem.at[i]) for i, (src, held, _) in enumerate(pairs)]
-    outs = [
-        pltpu.make_async_copy(held, dst, sem.at[2 + i]) for i, (_, held, dst) in enumerate(pairs)
-    ]
+    ins, outs = [], []
+    size = T // 4
+    for part in range(4):
+        rows_ = pl.ds(part * size, size)
+        for src, held, dst in ((a_ref, a_held, a_out), (b_ref, b_held, b_out)):
+            number = len(ins)
+            ins.append(pltpu.make_async_copy(src.at[rows_], held.at[rows_], sem.at[0, number]))
+            outs.append(pltpu.make_async_copy(held.at[rows_], dst.at[rows_], sem.at[1, number]))
     for move in ins:
         move.start()
-    for i in range(2):
-        ins[i].wait()
+    for i, move in enumerate(ins):
+        move.wait()
         outs[i].start()
     for move in outs:
         move.wait()
@@ -688,9 +665,8 @@
         pltpu.VMEM((T, ROWS), BF),
         pltpu.VMEM((T, ROWS), BF),
         pltpu.VMEM((8 * 1024, T), BF),
-        pltpu.VMEM((4, 2, 2, NX, T, T), BF),
-        pltpu.VMEM((16, NX, T, T), BF),
-        pltpu.VMEM((16, NX, T, T), BF),
+        pltpu.VMEM((4, 2, NX, 2, T, T), BF),
+        pltpu.VMEM((16, NX, 2, T, T), BF),
         pltpu.VMEM((HEADS, T, T), F32),
         pltpu.VMEM((HEADS, T, T), F32),
         pltpu.VMEM((NX, 2 * T + 32, T), BF),
@@ -759,7 +735,7 @@
         out_shape=tuple(jax.ShapeDtypeStruct(r.shape, r.dtype) for r in results),
         in_specs=[any_space, any_space],
         out_specs=(any_space, any_space),
-        scratch_shapes=[pltpu.VMEM((T, ROWS), BF), pltpu.VMEM((T, ROWS), BF), pltpu.SemaphoreType.DMA((4,))],
+        scratch_shapes=[pltpu.VMEM((T, ROWS), BF), pltpu.VMEM((T, ROWS), BF), pltpu.SemaphoreType.DMA((2, 8))],
     )(*results)
 
 

time: 61.4 us -> 61.5 us (level)
  no operation moved by 1% of the time
where the time goes in v4:
time: 61.5 us; the launch traced here: 60.8 us
  Pallas kernels  59.6 us (97%)
  between operations  1.29 us (2%)
    pallas_call x1, Pallas kernels, per_device(): pl.pallas_call(kernel, out_shape=(jax.ShapeDtypeStruct((T, ROWS), BF), ja...  57.7 us
    pallas_call x1, Pallas kernels, per_device(): pl.pallas_call(emit, out_shape=tuple((jax.ShapeDtypeStruct(r.shape, r.dty...  1.83 us

profile of v4, /device:TPU:16, one launch (start us, length us, event | category | flops | bytes accessed | tf_op | source)
XLA Modules:
  0.0 60.8 jit_solution(7386666062599934088)
XLA Ops:
  1.3 57.7 %shard_map.122 = (bf16[128,1024]{1,0:T(8,128)(2,1)}, bf16[128,1024]{1,0:T(8,128)(2,1)}) custom-call(bf16[128,1024]{1,0:T(8,128)(2,1)} %lq_hbm.1, bf16[128,1024]{1,0:T(8,128)(2,1)} %lk_hbm.1, bf16[128,1024]{1,0:T(8,128)(2,1)} %lv_hbm.1, f32[8,128]{1,0:T(8,128)} %ld_hbm.1, f32[8,128]{1,0:T(8,128)} %bitcast.5, bf16[128,1024]{1,0:T(8,128)(2,1)} %sq_hbm.1, ...), custom_call_target="tpu_custom_call" | custom-call | tf_op jit(solution)/shard_map/pallas_call | solution.py:708
  59.0 1.8 %shard_map.123 = (bf16[128,1024]{1,0:T(8,128)(2,1)}, bf16[128,1024]{1,0:T(8,128)(2,1)}) custom-call(bf16[128,1024]{1,0:T(8,128)(2,1)} %get-tuple-element.4.a_ref, bf16[128,1024]{1,0:T(8,128)(2,1)} %get-tuple-element.5.b_ref), custom_call_target="tpu_custom_call" | custom-call | tf_op jit(solution)/shard_map/pallas_call | solution.py:733
